TPU v7x, 32 devices: a whole 2x2x4 slice. The times are simulated.
32 devices in a mesh: dp: 8 (over z, x), tensor: 4 (over y, core).
Axes of the slice: x: 2, y: 2, z: 4, core: 2. Of those that a mesh axis runs over, the one named last changes fastest.
Arguments:
- attn_out: bfloat16 [8192, 8192], P('dp', 'tensor'), may hold values from -6 to 6
- out_grad: bfloat16 [8192, 4096], P('dp'), may hold values from -6 to 6
- completion_ids: int32 [8192], P('dp'), may hold values from 0 to 63, never falling along the last dimension, each value on 1 to 256 neighbouring positions
- rewards: float32 [64], replicated, may hold values from -6 to 6
- master: float32 [4096, 8192], P('dp', 'tensor'), may hold values from -0.0625 to 0.0625
- moment_one: float32 [4096, 8192], P('dp', 'tensor'), may hold values from -4 to 4
- moment_two: float32 [4096, 8192], P('dp', 'tensor'), may hold values from 0.05 to 0.5
Outputs:
- new_weights: bfloat16 [4096, 8192], P(None, 'tensor')
- new_one: float32 [4096, 8192], P('dp', 'tensor')
- new_two: float32 [4096, 8192], P('dp', 'tensor')
Inputs may be any that keep to these rules, and one draw needn't show every extreme that they name: `completion_ids`: completion numbers never fall along the tokens; every completion has 1 to 256 tokens and one has exactly 256.
All inputs are finite; a program needn't handle non-finite values.
Results may differ from a plain program's by a relative error of at most 0.013.
Values may be sent and summed in bfloat16 or wider, within the bound.
No kernel may reach another device: no remote copies, remote signals or barrier semaphores. Data moves between devices by JAX's collectives and lax.ppermute only.
A program may use at most 192 MiB of HBM per device.

v0:
```python
import jax
import jax.numpy as jnp
from jax import lax
from jax.sharding import PartitionSpec as P

GROUP = 8


beta_one = 0.9
beta_two = 0.95
learn_rate = 0.01
weight_decay = 0.1
epsilon = 1e-08
adam_step = 10.0


def token_weights(completion_ids, rewards):
    count_all = rewards.shape[0]
    onehot = (completion_ids[:, None] == jnp.arange(count_all, dtype=jnp.int32)[None, :]).astype(
        jnp.float32
    )
    lengths = lax.psum(jnp.sum(onehot, axis=0), "dp")
    grouped = rewards.reshape(count_all // GROUP, GROUP)
    center = jnp.mean(grouped, axis=1, keepdims=True)
    spread = jnp.sqrt(jnp.mean((grouped - center) * (grouped - center), axis=1, keepdims=True))
    advantage = ((grouped - center) / jnp.maximum(spread, 1.0)).reshape(-1)
    return jnp.dot(onehot, advantage / lengths, precision=lax.Precision.HIGHEST)


def contract_tokens(left, right):
    return lax.dot_general(
        left, right, (((0,), (0,)), ((), ())), preferred_element_type=jnp.float32
    )


def shards(attn_out, out_grad, completion_ids, rewards, master, moment_one, moment_two):
    token_weight = token_weights(completion_ids, rewards)
    weighted = (out_grad.astype(jnp.float32) * token_weight[:, None]).astype(jnp.bfloat16)
    grad = lax.psum_scatter(
        contract_tokens(weighted, attn_out).astype(jnp.bfloat16),
        "dp",
        scatter_dimension=0,
        tiled=True,
    ).astype(jnp.float32)
    new_one = beta_one * moment_one + (1.0 - beta_one) * grad
    new_two = beta_two * moment_two + (1.0 - beta_two) * grad * grad
    first = new_one / (1.0 - beta_one**adam_step)
    second = new_two / (1.0 - beta_two**adam_step)
    update = learn_rate * (first / (jnp.sqrt(second) + epsilon) + weight_decay * master)
    own_weights = (master - update).astype(jnp.bfloat16)
    new_weights = lax.all_gather(own_weights, "dp", axis=0, tiled=True)
    return (new_weights, new_one, new_two)


def solution(mesh):
    return jax.shard_map(
        shards,
        mesh=mesh,
        in_specs=(
            P("dp", "tensor"),
            P("dp", None),
            P("dp"),
            P(),
            P("dp", "tensor"),
            P("dp", "tensor"),
            P("dp", "tensor"),
        ),
        out_specs=(P(None, "tensor"), P("dp", "tensor"), P("dp", "tensor")),
        check_vma=False,
    )
```

profile of v0, /device:TPU:0, one launch (start us, length us, event | category | flops | bytes accessed | tf_op | source)
XLA Modules:
  0.0 595.5 jit_solution(5997712927654123008)
XLA Ops:
  7.2 0.0 reduce-scatter.2.cloned.1.call-start
  7.2 0.8 convert_reduce_fusion
  8.0 23.1 %psum.7 = f32[64]{0:T(128)S(1)} all-reduce(f32[64]{0:T(128)S(1)} %convert_reduce_fusion), channel_id=1, replica_groups=mesh['dp'=8,'tensor'=4] {'dp'}, use_global_device_ids=true, to_apply=%region_3.0 | all-reduce | flops 64 | bytes 512 | tf_op jit(solution)/shard_map/psum | solution.py:22
  31.1 0.7 reshape.26
  31.9 0.1 reduce_sum.27
  32.0 0.2 multiply_reduce_fusion
  32.2 0.1 div.35
  32.3 0.1 div.36
  32.3 0.1 sub.11
  32.4 0.1 sub.12
  32.5 0.9 fusion.3
  33.4 25.3 %convolution_convert_fusion = bf16[4096,2048]{1,0:T(8,128)(2,1)} fusion(bf16[1024,2048]{1,0:T(8,128)(2,1)} %param.7, bf16[1024,4096]{1,0:T(8,128)(2,1)} %param.8, f32[1024]{0:T(1024)S(1)} %bitcast.5), kind=kOutput, calls=%fused_computation.1 | convolution fusion | flops 17200840704 | bytes 29364224 | tf_op jit(solution)/shard_map/dot_general | solution.py:31
  58.7 0.0 reduce-scatter.2.cloned.1.call-update
  58.7 0.0 all-gather.2.cloned.1.call-start
  58.8 279.4 %reduce-scatter.2.cloned.1.call-done = bf16[512,2048]{1,0:T(8,128)(2,1)} async-done(((bf16[4096,2048]{1,0:T(8,128)(2,1)}), bf16[512,2048]{1,0:T(8,128)(2,1)}) %reduce-scatter.2.cloned.1.call-update) | async-done | bytes 2097168 | tf_op jit(solution)/shard_map/reduce_scatter | solution.py:39
  338.2 9.6 %subtract_convert_fusion = (bf16[512,2048]{1,0:T(8,128)(2,1)}, f32[512,2048]{1,0:T(8,128)}, f32[512,2048]{1,0:T(8,128)}) fusion(f32[512,2048]{1,0:T(8,128)} %param.11, bf16[512,2048]{1,0:T(8,128)(2,1)} %reduce-scatter.2.cloned.1.call-done, f32[512,2048]{1,0:T(8,128)} %param.12, f32[512,2048]{1,0:T(8,128)} %param.13), kind=kLoop, calls=%fused_computation.7 | loop fusion | flops 17825792 | bytes 25165824 | tf_op jit(solution)/shard_map/convert_element_type | solution.py:50
  347.7 0.0 all-gather.2.cloned.1.call-update
  347.8 226.8 %all-gather.2.cloned.1.call-done = bf16[4096,2048]{1,0:T(8,128)(2,1)} async-done(((bf16[512,2048]{1,0:T(8,128)(2,1)}), bf16[4096,2048]{1,0:T(8,128)(2,1)}) %all-gather.2.cloned.1.call-update) | async-done | bytes 16777232 | tf_op jit(solution)/shard_map/all_gather | solution.py:51
  574.5 14.2 %copy.11 = bf16[4096,2048]{1,0:T(8,128)(2,1)} copy(bf16[4096,2048]{1,0:T(8,128)(2,1)} %all-gather.2.cloned.1.call-done) | data formatting | bytes 33554432
  (2 shorter events, 0.0 us)
Async XLA Ops:
  7.2 331.0 %reduce-scatter.2.cloned.1.call-start = ((), (), s32[]{:S(2)}) async-start(), calls=%async_computation.1 | async-start | bytes 18874368 | tf_op jit(solution)/shard_map/reduce_scatter | solution.py:39
  58.7 515.8 %all-gather.2.cloned.1.call-start = ((), (), s32[]{:S(2)}) async-start(), calls=%async_computation.2 | async-start | bytes 18874368 | tf_op jit(solution)/shard_map/all_gather | solution.py:51
Sparse Core Ops, SparseCore 0:
  58.8 279.2 reduce-scatter.1
  347.9 226.5 all-gather.1
where the time goes:
time: 596 us
  waiting for transfers between devices  506 us (85%)
  matrix products  26.2 us (4%)
  blocking collectives  23.1 us (4%)
  local copies, waits for them, and re-layouts  15.2 us (3%)
  between operations  14 us (2%)
  other arithmetic  10.7 us (2%)
    reduce_scatter x1, waiting for transfers between devices, shards(): lax.psum_scatter(contract_tokens(weighted, attn_out).astype(jnp.bfloat16)...  279 us
    all_gather x1, waiting for transfers between devices, shards(): new_weights = lax.all_gather(own_weights, 'dp', axis=0, tiled=True)  227 us
    dot_general x1, matrix products, contract_tokens(): lax.dot_general(left, right, (((0,), (0,)), ((), ())), preferred_element_...  25.3 us
    psum x1, blocking collectives, token_weights(): lengths = lax.psum(jnp.sum(onehot, axis=0), 'dp')  23.1 us
    unnamed x1, local copies, waits for them, and re-layouts  14.2 us
  transfers between devices with their start and end apart: 2, of which 2 were waited for; matrix products, arithmetic and copies ran while one was open for 0% of the time, Pallas kernels for 0%

commit v1 on v0

v1 whole, which is shorter than its diff:
```python
import collections

import jax
import jax.numpy as jnp
from jax import lax
from jax.experimental.layout import Layout, with_layout_constraint
from jax.sharding import PartitionSpec as P

GROUP = 8
OUTER = 4
CHUNKS = 4
LAG = 2


beta_one = 0.9
beta_two = 0.95
learn_rate = 0.01
weight_decay = 0.1
epsilon = 1e-08
adam_step = 10.0


def token_weights(completion_ids, rewards, count):
    count_all = rewards.shape[0]
    onehot = (completion_ids[:, None] == jnp.arange(count_all, dtype=jnp.int32)[None, :]).astype(
        jnp.float32
    )
    own = jnp.sum(onehot, axis=0)
    before = lax.ppermute(own, "dp", [(d, d + 1) for d in range(count - 1)])
    after = lax.ppermute(own, "dp", [(d + 1, d) for d in range(count - 1)])
    lengths = jnp.maximum(own + before + after, 1.0)
    grouped = rewards.reshape(count_all // GROUP, GROUP)
    center = jnp.mean(grouped, axis=1, keepdims=True)
    spread = jnp.sqrt(jnp.mean((grouped - center) * (grouped - center), axis=1, keepdims=True))
    advantage = ((grouped - center) / jnp.maximum(spread, 1.0)).reshape(-1)
    return jnp.dot(onehot, advantage / lengths, precision=lax.Precision.HIGHEST)


def contract_tokens(left, right):
    return lax.dot_general(
        left, right, (((0,), (0,)), ((), ())), preferred_element_type=jnp.float32
    )


def straight(value):
    return with_layout_constraint(value, Layout(major_to_minor=(0, 1)))


def cycle(count):
    inner = count // OUTER
    walk = [o * inner for o in range(OUTER)]
    for turn, o in enumerate(reversed(range(OUTER))):
        along = range(1, inner) if turn % 2 == 0 else reversed(range(1, inner))
        walk += [o * inner + i for i in along]
    return walk


def shards(attn_out, out_grad, completion_ids, rewards, master, moment_one, moment_two):
    count = lax.psum(1, "dp")
    rows, wide = master.shape
    walk = cycle(count)
    place = [walk.index(d) for d in range(count)]
    me = lax.axis_index("dp")
    table = jnp.asarray(
        [[walk[(place[d] + k) % count] for k in range(count)] for d in range(count)], jnp.int32
    )[me]
    owners = [table[k] for k in range(count)]
    pairs = {
        turn: [(walk[p], walk[(p + turn) % count]) for p in range(count)] for turn in (1, -1)
    }
    token_weight = token_weights(completion_ids, rewards, count)
    part = wide // CHUNKS
    turns = [1 if index % 2 == 0 else -1 for index in range(CHUNKS)]
    cols = [slice(index * part, (index + 1) * part) for index in range(CHUNKS)]
    blocks = {}

    def weighted(k):
        k = k % count
        if k not in blocks:
            grads = lax.dynamic_slice(out_grad, (0, owners[k] * rows), (out_grad.shape[0], rows))
            blocks[k] = lax.optimization_barrier(
                (grads.astype(jnp.float32) * token_weight[:, None]).astype(jnp.bfloat16)
            )
        return blocks[k]

    def term(index, k):
        return contract_tokens(weighted(k), attn_out[:, cols[index]]).astype(jnp.bfloat16)

    moving = [straight(term(c, -turns[c])) for c in range(CHUNKS)]
    for step in range(1, count):
        for c, turn in enumerate(turns):
            arrived = lax.ppermute(moving[c], "dp", pairs[turn])
            moving[c] = arrived.astype(jnp.float32) + term(c, -turn * (step + 1)).astype(
                jnp.float32
            )
            if step < count - 1:
                moving[c] = straight(moving[c].astype(jnp.bfloat16))
    new_weights = jnp.zeros((count * rows, wide), jnp.bfloat16)
    ones, twos = [], []
    for c, grad in enumerate(moving):
        new_one = beta_one * moment_one[:, cols[c]] + (1.0 - beta_one) * grad
        new_two = beta_two * moment_two[:, cols[c]] + (1.0 - beta_two) * grad * grad
        first = new_one / (1.0 - beta_one**adam_step)
        second = new_two / (1.0 - beta_two**adam_step)
        update = learn_rate * (
            first / (jnp.sqrt(second) + epsilon) + weight_decay * master[:, cols[c]]
        )
        moving[c] = straight((master[:, cols[c]] - update).astype(jnp.bfloat16))
        ones.append(new_one)
        twos.append(new_two)
    waiting = collections.deque()

    def put(into):
        c, step, piece = waiting.popleft()
        at = owners[-turns[c] * step % count]
        return lax.dynamic_update_slice(into, piece, (at * rows, c * part))

    for step in range(count):
        for c, turn in enumerate(turns):
            waiting.append((c, step, moving[c]))
            if len(waiting) > LAG:
                new_weights = put(new_weights)
            if step < count - 1:
                moving[c], new_weights = lax.optimization_barrier((moving[c], new_weights))
                moving[c] = lax.ppermute(moving[c], "dp", pairs[turn])
    while waiting:
        new_weights = put(new_weights)
    return (new_weights, jnp.concatenate(ones, axis=1), jnp.concatenate(twos, axis=1))


def solution(mesh):
    return jax.shard_map(
        shards,
        mesh=mesh,
        in_specs=(
            P("dp", "tensor"),
            P("dp", None),
            P("dp"),
            P(),
            P("dp", "tensor"),
            P("dp", "tensor"),
            P("dp", "tensor"),
        ),
        out_specs=(P(None, "tensor"), P("dp", "tensor"), P("dp", "tensor")),
        check_vma=False,
    )
```

time: 596 us -> 373 us (0.63)
  waiting for transfers between devices: 506 us -> 241 us
  starting transfers between devices: 0.08 us -> 66.7 us
  blocking collectives: 23.1 us -> 0 us
  between operations: 14 us -> 6.41 us
    reduce_scatter x1 -> x0, waiting for transfers between devices: 279 us -> none  [shards(): lax.psum_scatter(contract_tokens(weighted, attn_out).astype(jnp.bfloat16)...]
    ppermute x0 -> x58, waiting for transfers between devices: none -> 241 us  [the longest x28 122 us: shards(): arrived = lax.ppermute(moving[c], 'dp', pairs[turn])]
    all_gather x1 -> x0, waiting for transfers between devices: 227 us -> none  [shards(): new_weights = lax.all_gather(own_weights, 'dp', axis=0, tiled=True)]
    ppermute x0 -> x58, starting transfers between devices: none -> 66.7 us  [the longest x28 31.6 us: shards(): arrived = lax.ppermute(moving[c], 'dp', pairs[turn])]
    psum x1 -> x0, blocking collectives: 23.1 us -> none  [token_weights(): lengths = lax.psum(jnp.sum(onehot, axis=0), 'dp')]
    unnamed x1 -> x10, local copies, waits for them, and re-layouts: 14.2 us -> 6.24 us
    dynamic_update_slice x0 -> x32, local copies, waits for them, and re-layouts: none -> 6.05 us  [put(): return lax.dynamic_update_slice(into, piece, (at * rows, c * part))]
    dot_general x1 -> x32, matrix products: 25.3 us -> 24.2 us  [contract_tokens(): lax.dot_general(left, right, (((0,), (0,)), ((), ())), preferred_element_...]
  transfers between devices with their start and end apart: 2 -> 58, of which waited for: 2 -> 46; matrix products, arithmetic and copies ran while one was open for 0% -> 7% of each run, Pallas kernels for 0% -> 0%
where the time goes in v1:
time: 373 us; the launch traced here: 372 us
  waiting for transfers between devices  241 us (65%)
  starting transfers between devices  66.7 us (18%)
  matrix products  25.1 us (7%)
  local copies, waits for them, and re-layouts  16.8 us (5%)
  other arithmetic  16.5 us (4%)
  between operations  6.41 us (2%)
    ppermute x28, waiting for transfers between devices, shards(): arrived = lax.ppermute(moving[c], 'dp', pairs[turn])  122 us
    ppermute x28, waiting for transfers between devices, shards(): moving[c] = lax.ppermute(moving[c], 'dp', pairs[turn])  119 us
    ppermute x28, starting transfers between devices, shards(): arrived = lax.ppermute(moving[c], 'dp', pairs[turn])  31.6 us
    ppermute x28, starting transfers between devices, shards(): moving[c] = lax.ppermute(moving[c], 'dp', pairs[turn])  28.9 us
    dot_general x32, matrix products, contract_tokens(): lax.dot_general(left, right, (((0,), (0,)), ((), ())), preferred_element_...  24.2 us
  transfers between devices with their start and end apart: 58, of which 46 were waited for; matrix products, arithmetic and copies ran while one was open for 7% of the time, Pallas kernels for 0%

profile of v1, /device:TPU:0, one launch (start us, length us, event | category | flops | bytes accessed | tf_op | source)
XLA Modules:
  0.0 372.2 jit_solution(4176379103529465956)
XLA Ops:
  47.6 8.4 %collective-permute-done.2 = bf16[512,512]{1,0:T(8,128)(2,1)S(1)} collective-permute-done((bf16[512,512]{1,0:T(8,128)(2,1)S(1)}, bf16[512,512]{1,0:T(8,128)(2,1)S(1)}, u32[]{:S(2)}, u32[]{:S(2)}) %collective-permute-start.2) | collective-permute-done | bytes 524320 | tf_op jit(solution)/shard_map/ppermute | solution.py:92
  59.7 9.4 %collective-permute-done.23 = bf16[512,512]{1,0:T(8,128)(2,1)S(1)} collective-permute-done((bf16[512,512]{1,0:T(8,128)(2,1)S(1)}, bf16[512,512]{1,0:T(8,128)(2,1)S(1)}, u32[]{:S(2)}, u32[]{:S(2)}) %collective-permute-start.23) | collective-permute-done | bytes 524320 | tf_op jit(solution)/shard_map/ppermute | solution.py:92
  81.6 10.0 %collective-permute-done.24 = bf16[512,512]{1,0:T(8,128)(2,1)S(1)} collective-permute-done((bf16[512,512]{1,0:T(8,128)(2,1)S(1)}, bf16[512,512]{1,0:T(8,128)(2,1)S(1)}, u32[]{:S(2)}, u32[]{:S(2)}) %collective-permute-start.24) | collective-permute-done | bytes 524320 | tf_op jit(solution)/shard_map/ppermute | solution.py:92
  94.1 6.9 %collective-permute-done.4 = bf16[512,512]{1,0:T(8,128)(2,1)S(1)} collective-permute-done((bf16[512,512]{1,0:T(8,128)(2,1)S(1)}, bf16[512,512]{1,0:T(8,128)(2,1)S(1)}, u32[]{:S(2)}, u32[]{:S(2)}) %collective-permute-start.4) | collective-permute-done | bytes 524320 | tf_op jit(solution)/shard_map/ppermute | solution.py:92
  104.1 10.0 %collective-permute-done.25 = bf16[512,512]{1,0:T(8,128)(2,1)S(1)} collective-permute-done((bf16[512,512]{1,0:T(8,128)(2,1)S(1)}, bf16[512,512]{1,0:T(8,128)(2,1)S(1)}, u32[]{:S(2)}, u32[]{:S(2)}) %collective-permute-start.25) | collective-permute-done | bytes 524320 | tf_op jit(solution)/shard_map/ppermute | solution.py:92
  116.5 6.9 %collective-permute-done.5 = bf16[512,512]{1,0:T(8,128)(2,1)S(1)} collective-permute-done((bf16[512,512]{1,0:T(8,128)(2,1)S(1)}, bf16[512,512]{1,0:T(8,128)(2,1)S(1)}, u32[]{:S(2)}, u32[]{:S(2)}) %collective-permute-start.5) | collective-permute-done | bytes 524320 | tf_op jit(solution)/shard_map/ppermute | solution.py:92
  126.5 10.0 %collective-permute-done.26 = bf16[512,512]{1,0:T(8,128)(2,1)S(1)} collective-permute-done((bf16[512,512]{1,0:T(8,128)(2,1)S(1)}, bf16[512,512]{1,0:T(8,128)(2,1)S(1)}, u32[]{:S(2)}, u32[]{:S(2)}) %collective-permute-start.26) | collective-permute-done | bytes 524320 | tf_op jit(solution)/shard_map/ppermute | solution.py:92
  139.0 6.9 %collective-permute-done.6 = bf16[512,512]{1,0:T(8,128)(2,1)S(1)} collective-permute-done((bf16[512,512]{1,0:T(8,128)(2,1)S(1)}, bf16[512,512]{1,0:T(8,128)(2,1)S(1)}, u32[]{:S(2)}, u32[]{:S(2)}) %collective-permute-start.6) | collective-permute-done | bytes 524320 | tf_op jit(solution)/shard_map/ppermute | solution.py:92
  149.0 10.0 %collective-permute-done.27 = bf16[512,512]{1,0:T(8,128)(2,1)S(1)} collective-permute-done((bf16[512,512]{1,0:T(8,128)(2,1)S(1)}, bf16[512,512]{1,0:T(8,128)(2,1)S(1)}, u32[]{:S(2)}, u32[]{:S(2)}) %collective-permute-start.27) | collective-permute-done | bytes 524320 | tf_op jit(solution)/shard_map/ppermute | solution.py:92
  161.5 6.9 %collective-permute-done.7 = bf16[512,512]{1,0:T(8,128)(2,1)S(1)} collective-permute-done((bf16[512,512]{1,0:T(8,128)(2,1)S(1)}, bf16[512,512]{1,0:T(8,128)(2,1)S(1)}, u32[]{:S(2)}, u32[]{:S(2)}) %collective-permute-start.7) | collective-permute-done | bytes 524320 | tf_op jit(solution)/shard_map/ppermute | solution.py:92
  171.5 10.0 %collective-permute-done.28 = bf16[512,512]{1,0:T(8,128)(2,1)S(1)} collective-permute-done((bf16[512,512]{1,0:T(8,128)(2,1)S(1)}, bf16[512,512]{1,0:T(8,128)(2,1)S(1)}, u32[]{:S(2)}, u32[]{:S(2)}) %collective-permute-start.28) | collective-permute-done | bytes 524320 | tf_op jit(solution)/shard_map/ppermute | solution.py:92
  184.7 6.2 %collective-permute-done.8 = bf16[512,512]{1,0:T(8,128)(2,1)S(1)} collective-permute-done((bf16[512,512]{1,0:T(8,128)(2,1)S(1)}, bf16[512,512]{1,0:T(8,128)(2,1)S(1)}, u32[]{:S(2)}, u32[]{:S(2)}) %collective-permute-start.8) | collective-permute-done | bytes 524320 | tf_op jit(solution)/shard_map/ppermute | solution.py:92
  192.7 9.2 %collective-permute-done.29 = bf16[512,512]{1,0:T(8,128)(2,1)S(1)} collective-permute-done((bf16[512,512]{1,0:T(8,128)(2,1)S(1)}, bf16[512,512]{1,0:T(8,128)(2,1)S(1)}, u32[]{:S(2)}, u32[]{:S(2)}) %collective-permute-start.29) | collective-permute-done | bytes 524320 | tf_op jit(solution)/shard_map/ppermute | solution.py:92
  212.5 7.4 %collective-permute-done.33 = bf16[512,512]{1,0:T(8,128)(2,1)S(1)} collective-permute-done((bf16[512,512]{1,0:T(8,128)(2,1)S(1)}, bf16[512,512]{1,0:T(8,128)(2,1)S(1)}, u32[]{:S(2)}, u32[]{:S(2)}) %collective-permute-start.33) | collective-permute-done | bytes 524320 | tf_op jit(solution)/shard_map/ppermute | solution.py:125
  223.0 8.1 %collective-permute-done.31 = bf16[512,512]{1,0:T(8,128)(2,1)S(1)} collective-permute-done((bf16[512,512]{1,0:T(8,128)(2,1)S(1)}, bf16[512,512]{1,0:T(8,128)(2,1)S(1)}, u32[]{:S(2)}, u32[]{:S(2)}) %collective-permute-start.31) | collective-permute-done | bytes 524320 | tf_op jit(solution)/shard_map/ppermute | solution.py:125
  234.2 8.1 %collective-permute-done.37 = bf16[512,512]{1,0:T(8,128)(2,1)S(1)} collective-permute-done((bf16[512,512]{1,0:T(8,128)(2,1)S(1)}, bf16[512,512]{1,0:T(8,128)(2,1)S(1)}, u32[]{:S(2)}, u32[]{:S(2)}) %collective-permute-start.37) | collective-permute-done | bytes 524320 | tf_op jit(solution)/shard_map/ppermute | solution.py:125
  245.5 8.1 %collective-permute-done.35 = bf16[512,512]{1,0:T(8,128)(2,1)S(1)} collective-permute-done((bf16[512,512]{1,0:T(8,128)(2,1)S(1)}, bf16[512,512]{1,0:T(8,128)(2,1)S(1)}, u32[]{:S(2)}, u32[]{:S(2)}) %collective-permute-start.35) | collective-permute-done | bytes 524320 | tf_op jit(solution)/shard_map/ppermute | solution.py:125
  256.7 8.1 %collective-permute-done.41 = bf16[512,512]{1,0:T(8,128)(2,1)S(1)} collective-permute-done((bf16[512,512]{1,0:T(8,128)(2,1)S(1)}, bf16[512,512]{1,0:T(8,128)(2,1)S(1)}, u32[]{:S(2)}, u32[]{:S(2)}) %collective-permute-start.41) | collective-permute-done | bytes 524320 | tf_op jit(solution)/shard_map/ppermute | solution.py:125
  268.0 8.1 %collective-permute-done.39 = bf16[512,512]{1,0:T(8,128)(2,1)S(1)} collective-permute-done((bf16[512,512]{1,0:T(8,128)(2,1)S(1)}, bf16[512,512]{1,0:T(8,128)(2,1)S(1)}, u32[]{:S(2)}, u32[]{:S(2)}) %collective-permute-start.39) | collective-permute-done | bytes 524320 | tf_op jit(solution)/shard_map/ppermute | solution.py:125
  279.2 8.1 %collective-permute-done.45 = bf16[512,512]{1,0:T(8,128)(2,1)S(1)} collective-permute-done((bf16[512,512]{1,0:T(8,128)(2,1)S(1)}, bf16[512,512]{1,0:T(8,128)(2,1)S(1)}, u32[]{:S(2)}, u32[]{:S(2)}) %collective-permute-start.45) | collective-permute-done | bytes 524320 | tf_op jit(solution)/shard_map/ppermute | solution.py:125
  290.4 8.1 %collective-permute-done.43 = bf16[512,512]{1,0:T(8,128)(2,1)S(1)} collective-permute-done((bf16[512,512]{1,0:T(8,128)(2,1)S(1)}, bf16[512,512]{1,0:T(8,128)(2,1)S(1)}, u32[]{:S(2)}, u32[]{:S(2)}) %collective-permute-start.43) | collective-permute-done | bytes 524320 | tf_op jit(solution)/shard_map/ppermute | solution.py:125
  301.7 8.1 %collective-permute-done.49 = bf16[512,512]{1,0:T(8,128)(2,1)S(1)} collective-permute-done((bf16[512,512]{1,0:T(8,128)(2,1)S(1)}, bf16[512,512]{1,0:T(8,128)(2,1)S(1)}, u32[]{:S(2)}, u32[]{:S(2)}) %collective-permute-start.49) | collective-permute-done | bytes 524320 | tf_op jit(solution)/shard_map/ppermute | solution.py:125
  328.2 7.1 %collective-permute-done.53 = bf16[512,512]{1,0:T(8,128)(2,1)} collective-permute-done((bf16[512,512]{1,0:T(8,128)(2,1)S(1)}, bf16[512,512]{1,0:T(8,128)(2,1)}, u32[]{:S(2)}, u32[]{:S(2)}) %collective-permute-start.53) | collective-permute-done | bytes 524320 | tf_op jit(solution)/shard_map/ppermute | solution.py:125
  338.6 8.0 %collective-permute-done.51 = bf16[512,512]{1,0:T(8,128)(2,1)} collective-permute-done((bf16[512,512]{1,0:T(8,128)(2,1)S(1)}, bf16[512,512]{1,0:T(8,128)(2,1)}, u32[]{:S(2)}, u32[]{:S(2)}) %collective-permute-start.51) | collective-permute-done | bytes 524320 | tf_op jit(solution)/shard_map/ppermute | solution.py:125
  (204 shorter events, 167.1 us)
Async XLA Ops:
  44.0 25.1 %collective-permute-start.23 = (bf16[512,512]{1,0:T(8,128)(2,1)S(1)}, bf16[512,512]{1,0:T(8,128)(2,1)S(1)}, u32[]{:S(2)}, u32[]{:S(2)}) collective-permute-start(bf16[512,512]{1,0:T(8,128)(2,1)S(1)} %convolution_convert_fusion.7), channel_id=1, source_target_pairs={{0,8},{8,16},{16,24},{24,28},{28,20},{20,12},{12,4},{4,0},{1,9},{9... | collective-permute-start | bytes 1572872 | tf_op jit(solution)/shard_map/ppermute | solution.py:92
  46.1 24.9 %collective-permute-start.16 = (bf16[512,512]{1,0:T(8,128)(2,1)S(1)}, bf16[512,512]{1,0:T(8,128)(2,1)S(1)}, u32[]{:S(2)}, u32[]{:S(2)}) collective-permute-start(bf16[512,512]{1,0:T(8,128)(2,1)S(1)} %convolution_convert_fusion.15), channel_id=1, source_target_pairs={{0,4},{8,0},{16,8},{24,16},{28,24},{20,28},{12,20},{4,12},{1,5},{9... | collective-permute-start | bytes 1572872 | tf_op jit(solution)/shard_map/ppermute | solution.py:92
  80.5 22.3 %collective-permute-start.11 = (bf16[512,512]{1,0:T(8,128)(2,1)S(1)}, bf16[512,512]{1,0:T(8,128)(2,1)S(1)}, u32[]{:S(2)}, u32[]{:S(2)}) collective-permute-start(bf16[512,512]{1,0:T(8,128)(2,1)S(1)} %add_convert_fusion.16), channel_id=1, source_target_pairs={{0,8},{8,16},{16,24},{24,28},{28,20},{20,12},{12,4},{4,0},{1,9},{9... | collective-permute-start | bytes 1572872 | tf_op jit(solution)/shard_map/ppermute | solution.py:92
  101.2 22.3 %collective-permute-start.5 = (bf16[512,512]{1,0:T(8,128)(2,1)S(1)}, bf16[512,512]{1,0:T(8,128)(2,1)S(1)}, u32[]{:S(2)}, u32[]{:S(2)}) collective-permute-start(bf16[512,512]{1,0:T(8,128)(2,1)S(1)} %add_convert_fusion.21), channel_id=1, source_target_pairs={{0,4},{8,0},{16,8},{24,16},{28,24},{20,28},{12,20},{4,12},{1,5},{9... | collective-permute-start | bytes 1572872 | tf_op jit(solution)/shard_map/ppermute | solution.py:92
  114.2 22.3 %collective-permute-start.26 = (bf16[512,512]{1,0:T(8,128)(2,1)S(1)}, bf16[512,512]{1,0:T(8,128)(2,1)S(1)}, u32[]{:S(2)}, u32[]{:S(2)}) collective-permute-start(bf16[512,512]{1,0:T(8,128)(2,1)S(1)} %add_convert_fusion.3), channel_id=1, source_target_pairs={{0,8},{8,16},{16,24},{24,28},{28,20},{20,12},{12,4},{4,0},{1,9},{9... | collective-permute-start | bytes 1572872 | tf_op jit(solution)/shard_map/ppermute | solution.py:92
  160.4 23.1 %collective-permute-start.21 = (bf16[512,512]{1,0:T(8,128)(2,1)S(1)}, bf16[512,512]{1,0:T(8,128)(2,1)S(1)}, u32[]{:S(2)}, u32[]{:S(2)}) collective-permute-start(bf16[512,512]{1,0:T(8,128)(2,1)S(1)} %add_convert_fusion.7), channel_id=1, source_target_pairs={{0,4},{8,0},{16,8},{24,16},{28,24},{20,28},{12,20},{4,12},{1,5},{9... | collective-permute-start | bytes 1572872 | tf_op jit(solution)/shard_map/ppermute | solution.py:92
  183.6 22.7 %collective-permute-start.22 = (bf16[512,512]{1,0:T(8,128)(2,1)S(1)}, bf16[512,512]{1,0:T(8,128)(2,1)S(1)}, u32[]{:S(2)}, u32[]{:S(2)}) collective-permute-start(bf16[512,512]{1,0:T(8,128)(2,1)S(1)} %add_convert_fusion.6), channel_id=1, source_target_pairs={{0,4},{8,0},{16,8},{24,16},{28,24},{20,28},{12,20},{4,12},{1,5},{9... | collective-permute-start | bytes 1572872 | tf_op jit(solution)/shard_map/ppermute | solution.py:92
  219.9 22.5 %collective-permute-start.37 = (bf16[512,512]{1,0:T(8,128)(2,1)S(1)}, bf16[512,512]{1,0:T(8,128)(2,1)S(1)}, u32[]{:S(2)}, u32[]{:S(2)}) collective-permute-start(bf16[512,512]{1,0:T(8,128)(2,1)S(1)} %collective-permute-done.33), channel_id=1, source_target_pairs={{0,8},{8,16},{16,24},{24,28},{28,20},{20,12},{12,4},{4,0},{1,9},{9... | collective-permute-start | bytes 1572872 | tf_op jit(solution)/shard_map/ppermute | solution.py:125
  222.2 22.5 %collective-permute-start.36 = (bf16[512,512]{1,0:T(8,128)(2,1)S(1)}, bf16[512,512]{1,0:T(8,128)(2,1)S(1)}, u32[]{:S(2)}, u32[]{:S(2)}) collective-permute-start(bf16[512,512]{1,0:T(8,128)(2,1)S(1)} %collective-permute-done.32), channel_id=1, source_target_pairs={{0,4},{8,0},{16,8},{24,16},{28,24},{20,28},{12,20},{4,12},{1,5},{9... | collective-permute-start | bytes 1572872 | tf_op jit(solution)/shard_map/ppermute | solution.py:125
  231.2 22.5 %collective-permute-start.35 = (bf16[512,512]{1,0:T(8,128)(2,1)S(1)}, bf16[512,512]{1,0:T(8,128)(2,1)S(1)}, u32[]{:S(2)}, u32[]{:S(2)}) collective-permute-start(bf16[512,512]{1,0:T(8,128)(2,1)S(1)} %collective-permute-done.31), channel_id=1, source_target_pairs={{0,8},{8,16},{16,24},{24,28},{28,20},{20,12},{12,4},{4,0},{1,9},{9... | collective-permute-start | bytes 1572872 | tf_op jit(solution)/shard_map/ppermute | solution.py:125
  233.4 22.5 %collective-permute-start.34 = (bf16[512,512]{1,0:T(8,128)(2,1)S(1)}, bf16[512,512]{1,0:T(8,128)(2,1)S(1)}, u32[]{:S(2)}, u32[]{:S(2)}) collective-permute-start(bf16[512,512]{1,0:T(8,128)(2,1)S(1)} %collective-permute-done.30), channel_id=1, source_target_pairs={{0,4},{8,0},{16,8},{24,16},{28,24},{20,28},{12,20},{4,12},{1,5},{9... | collective-permute-start | bytes 1572872 | tf_op jit(solution)/shard_map/ppermute | solution.py:125
  242.4 22.5 %collective-permute-start.41 = (bf16[512,512]{1,0:T(8,128)(2,1)S(1)}, bf16[512,512]{1,0:T(8,128)(2,1)S(1)}, u32[]{:S(2)}, u32[]{:S(2)}) collective-permute-start(bf16[512,512]{1,0:T(8,128)(2,1)S(1)} %collective-permute-done.37), channel_id=1, source_target_pairs={{0,8},{8,16},{16,24},{24,28},{28,20},{20,12},{12,4},{4,0},{1,9},{9... | collective-permute-start | bytes 1572872 | tf_op jit(solution)/shard_map/ppermute | solution.py:125
  244.7 22.5 %collective-permute-start.40 = (bf16[512,512]{1,0:T(8,128)(2,1)S(1)}, bf16[512,512]{1,0:T(8,128)(2,1)S(1)}, u32[]{:S(2)}, u32[]{:S(2)}) collective-permute-start(bf16[512,512]{1,0:T(8,128)(2,1)S(1)} %collective-permute-done.36), channel_id=1, source_target_pairs={{0,4},{8,0},{16,8},{24,16},{28,24},{20,28},{12,20},{4,12},{1,5},{9... | collective-permute-start | bytes 1572872 | tf_op jit(solution)/shard_map/ppermute | solution.py:125
  253.6 22.5 %collective-permute-start.39 = (bf16[512,512]{1,0:T(8,128)(2,1)S(1)}, bf16[512,512]{1,0:T(8,128)(2,1)S(1)}, u32[]{:S(2)}, u32[]{:S(2)}) collective-permute-start(bf16[512,512]{1,0:T(8,128)(2,1)S(1)} %collective-permute-done.35), channel_id=1, source_target_pairs={{0,8},{8,16},{16,24},{24,28},{28,20},{20,12},{12,4},{4,0},{1,9},{9... | collective-permute-start | bytes 1572872 | tf_op jit(solution)/shard_map/ppermute | solution.py:125
  255.9 22.5 %collective-permute-start.38 = (bf16[512,512]{1,0:T(8,128)(2,1)S(1)}, bf16[512,512]{1,0:T(8,128)(2,1)S(1)}, u32[]{:S(2)}, u32[]{:S(2)}) collective-permute-start(bf16[512,512]{1,0:T(8,128)(2,1)S(1)} %collective-permute-done.34), channel_id=1, source_target_pairs={{0,4},{8,0},{16,8},{24,16},{28,24},{20,28},{12,20},{4,12},{1,5},{9... | collective-permute-start | bytes 1572872 | tf_op jit(solution)/shard_map/ppermute | solution.py:125
  264.9 22.5 %collective-permute-start.45 = (bf16[512,512]{1,0:T(8,128)(2,1)S(1)}, bf16[512,512]{1,0:T(8,128)(2,1)S(1)}, u32[]{:S(2)}, u32[]{:S(2)}) collective-permute-start(bf16[512,512]{1,0:T(8,128)(2,1)S(1)} %collective-permute-done.41), channel_id=1, source_target_pairs={{0,8},{8,16},{16,24},{24,28},{28,20},{20,12},{12,4},{4,0},{1,9},{9... | collective-permute-start | bytes 1572872 | tf_op jit(solution)/shard_map/ppermute | solution.py:125
  267.1 22.5 %collective-permute-start.44 = (bf16[512,512]{1,0:T(8,128)(2,1)S(1)}, bf16[512,512]{1,0:T(8,128)(2,1)S(1)}, u32[]{:S(2)}, u32[]{:S(2)}) collective-permute-start(bf16[512,512]{1,0:T(8,128)(2,1)S(1)} %collective-permute-done.40), channel_id=1, source_target_pairs={{0,4},{8,0},{16,8},{24,16},{28,24},{20,28},{12,20},{4,12},{1,5},{9... | collective-permute-start | bytes 1572872 | tf_op jit(solution)/shard_map/ppermute | solution.py:125
  276.1 22.5 %collective-permute-start.43 = (bf16[512,512]{1,0:T(8,128)(2,1)S(1)}, bf16[512,512]{1,0:T(8,128)(2,1)S(1)}, u32[]{:S(2)}, u32[]{:S(2)}) collective-permute-start(bf16[512,512]{1,0:T(8,128)(2,1)S(1)} %collective-permute-done.39), channel_id=1, source_target_pairs={{0,8},{8,16},{16,24},{24,28},{28,20},{20,12},{12,4},{4,0},{1,9},{9... | collective-permute-start | bytes 1572872 | tf_op jit(solution)/shard_map/ppermute | solution.py:125
  278.4 22.5 %collective-permute-start.42 = (bf16[512,512]{1,0:T(8,128)(2,1)S(1)}, bf16[512,512]{1,0:T(8,128)(2,1)S(1)}, u32[]{:S(2)}, u32[]{:S(2)}) collective-permute-start(bf16[512,512]{1,0:T(8,128)(2,1)S(1)} %collective-permute-done.38), channel_id=1, source_target_pairs={{0,4},{8,0},{16,8},{24,16},{28,24},{20,28},{12,20},{4,12},{1,5},{9... | collective-permute-start | bytes 1572872 | tf_op jit(solution)/shard_map/ppermute | solution.py:125
  287.3 22.5 %collective-permute-start.49 = (bf16[512,512]{1,0:T(8,128)(2,1)S(1)}, bf16[512,512]{1,0:T(8,128)(2,1)S(1)}, u32[]{:S(2)}, u32[]{:S(2)}) collective-permute-start(bf16[512,512]{1,0:T(8,128)(2,1)S(1)} %collective-permute-done.45), channel_id=1, source_target_pairs={{0,8},{8,16},{16,24},{24,28},{28,20},{20,12},{12,4},{4,0},{1,9},{9... | collective-permute-start | bytes 1572872 | tf_op jit(solution)/shard_map/ppermute | solution.py:125
  289.6 22.5 %collective-permute-start.48 = (bf16[512,512]{1,0:T(8,128)(2,1)S(1)}, bf16[512,512]{1,0:T(8,128)(2,1)S(1)}, u32[]{:S(2)}, u32[]{:S(2)}) collective-permute-start(bf16[512,512]{1,0:T(8,128)(2,1)S(1)} %collective-permute-done.44), channel_id=1, source_target_pairs={{0,4},{8,0},{16,8},{24,16},{28,24},{20,28},{12,20},{4,12},{1,5},{9... | collective-permute-start | bytes 1572872 | tf_op jit(solution)/shard_map/ppermute | solution.py:125
  322.4 24.2 %collective-permute-start.51 = (bf16[512,512]{1,0:T(8,128)(2,1)S(1)}, bf16[512,512]{1,0:T(8,128)(2,1)}, u32[]{:S(2)}, u32[]{:S(2)}) collective-permute-start(bf16[512,512]{1,0:T(8,128)(2,1)S(1)} %collective-permute-done.47), channel_id=1, source_target_pairs={{0,8},{8,16},{16,24},{24,28},{28,20},{20,12},{12,4},{4,0},{1,9},{9... | collective-permute-start | bytes 1572872 | tf_op jit(solution)/shard_map/ppermute | solution.py:125
  323.9 25.3 %collective-permute-start.50 = (bf16[512,512]{1,0:T(8,128)(2,1)S(1)}, bf16[512,512]{1,0:T(8,128)(2,1)}, u32[]{:S(2)}, u32[]{:S(2)}) collective-permute-start(bf16[512,512]{1,0:T(8,128)(2,1)S(1)} %collective-permute-done.46), channel_id=1, source_target_pairs={{0,4},{8,0},{16,8},{24,16},{28,24},{20,28},{12,20},{4,12},{1,5},{9... | collective-permute-start | bytes 1572872 | tf_op jit(solution)/shard_map/ppermute | solution.py:125
  335.3 22.4 %collective-permute-start.54 = (bf16[512,512]{1,0:T(8,128)(2,1)}, bf16[512,512]{1,0:T(8,128)(2,1)S(1)}, u32[]{:S(2)}, u32[]{:S(2)}) collective-permute-start(bf16[512,512]{1,0:T(8,128)(2,1)} %collective-permute-done.53), channel_id=1, source_target_pairs={{0,8},{8,16},{16,24},{24,28},{28,20},{20,12},{12,4},{4,0},{1,9},{9... | collective-permute-start | bytes 1572872 | tf_op jit(solution)/shard_map/ppermute | solution.py:125
  (39 other events, 758.3 us)

commit v2 on v1

--- a/solution.py
+++ b/solution.py
@@ -10,6 +10,7 @@
 OUTER = 4
 CHUNKS = 4
 LAG = 2
+AHEAD = 3
 
 
 beta_one = 0.9
@@ -74,30 +75,54 @@
     cols = [slice(index * part, (index + 1) * part) for index in range(CHUNKS)]
     blocks = {}
 
-    def weighted(k):
-        k = k % count
-        if k not in blocks:
-            grads = lax.dynamic_slice(out_grad, (0, owners[k] * rows), (out_grad.shape[0], rows))
-            blocks[k] = lax.optimization_barrier(
-                (grads.astype(jnp.float32) * token_weight[:, None]).astype(jnp.bfloat16)
-            )
-        return blocks[k]
+    def weighted(k, gate):
+        grads = lax.dynamic_slice(out_grad, (0, owners[k] * rows), (out_grad.shape[0], rows))
+        return (grads.astype(jnp.float32) * gate[:, None]).astype(jnp.bfloat16)
 
-    def term(index, k):
-        return contract_tokens(weighted(k), attn_out[:, cols[index]]).astype(jnp.bfloat16)
+    def term(c, step):
+        left = blocks[-turns[c] * step % count]
+        value = contract_tokens(left, attn_out[:, cols[c]])
+        return straight(value.astype(jnp.bfloat16))
 
-    moving = [straight(term(c, -turns[c])) for c in range(CHUNKS)]
-    for step in range(1, count):
-        for c, turn in enumerate(turns):
-            arrived = lax.ppermute(moving[c], "dp", pairs[turn])
-            moving[c] = arrived.astype(jnp.float32) + term(c, -turn * (step + 1)).astype(
-                jnp.float32
-            )
-            if step < count - 1:
-                moving[c] = straight(moving[c].astype(jnp.bfloat16))
+    gate = token_weight
+    for turn in (1, -1):
+        blocks[-turn % count] = weighted(-turn % count, gate)
+    moving = []
+    for c in range(CHUNKS):
+        value, gate = lax.optimization_barrier((term(c, 1), gate))
+        moving.append(value)
+    events = [(step, c) for step in range(1, count) for c in range(CHUNKS)]
+    terms = {}
+
+    def prepare(number, gate):
+        if number < len(events):
+            step, c = events[number]
+            k = -turns[c] * (step + 1) % count
+            if k not in blocks:
+                blocks[k] = weighted(k, gate)
+            blocks[k], gate = lax.optimization_barrier((blocks[k], gate))
+            terms[number] = term(c, step + 1)
+        return gate
+
+    for number, (step, c) in enumerate(events):
+        arrived = lax.ppermute(moving[c], "dp", pairs[turns[c]])
+        if number == 0:
+            gate = prepare(0, gate)
+        arrived, gate = lax.optimization_barrier((arrived, gate))
+        if number == 0:
+            for early in range(1, AHEAD):
+                gate = prepare(early, gate)
+        moving[c] = arrived.astype(jnp.float32) + terms.pop(number).astype(jnp.float32)
+        if step < count - 1:
+            moving[c] = straight(moving[c].astype(jnp.bfloat16))
+        moving[c], gate = lax.optimization_barrier((moving[c], gate))
+        gate = prepare(number + AHEAD, gate)
     new_weights = jnp.zeros((count * rows, wide), jnp.bfloat16)
     ones, twos = [], []
-    for c, grad in enumerate(moving):
+    for c in range(CHUNKS):
+        grad = moving[c]
+        if c:
+            grad, moving[c - 1] = lax.optimization_barrier((grad, moving[c - 1]))
         new_one = beta_one * moment_one[:, cols[c]] + (1.0 - beta_one) * grad
         new_two = beta_two * moment_two[:, cols[c]] + (1.0 - beta_two) * grad * grad
         first = new_one / (1.0 - beta_one**adam_step)
@@ -108,6 +133,7 @@
         moving[c] = straight((master[:, cols[c]] - update).astype(jnp.bfloat16))
         ones.append(new_one)
         twos.append(new_two)
+    new_one, new_two = jnp.concatenate(ones, axis=1), jnp.concatenate(twos, axis=1)
     waiting = collections.deque()
 
     def put(into):
@@ -116,6 +142,10 @@
         return lax.dynamic_update_slice(into, piece, (at * rows, c * part))
 
     for step in range(count):
+        if step == 3:
+            new_weights, new_one, new_two = lax.optimization_barrier(
+                (new_weights, new_one, new_two)
+            )
         for c, turn in enumerate(turns):
             waiting.append((c, step, moving[c]))
             if len(waiting) > LAG:
@@ -125,7 +155,7 @@
                 moving[c] = lax.ppermute(moving[c], "dp", pairs[turn])
     while waiting:
         new_weights = put(new_weights)
-    return (new_weights, jnp.concatenate(ones, axis=1), jnp.concatenate(twos, axis=1))
+    return (new_weights, new_one, new_two)
 
 
 def solution(mesh):

time: 373 us -> 357 us (0.957)
  waiting for transfers between devices: 241 us -> 224 us
    ppermute x28, waiting for transfers between devices: 122 us -> 112 us  [shards(): arrived = lax.ppermute(moving[c], 'dp', pairs[turns[c]])]
    ppermute x28, waiting for transfers between devices: 119 us -> 111 us  [shards(): moving[c] = lax.ppermute(moving[c], 'dp', pairs[turn])]
  transfers between devices with their start and end apart: 58 -> 58, of which waited for: 46 -> 47; matrix products, arithmetic and copies ran while one was open for 7% -> 11% of each run, Pallas kernels for 0% -> 0%
where the time goes in v2:
time: 357 us; the launch traced here: 356 us
  waiting for transfers between devices  224 us (63%)
  starting transfers between devices  66.6 us (19%)
  matrix products  24.4 us (7%)
  local copies, waits for them, and re-layouts  17.7 us (5%)
  other arithmetic  17.2 us (5%)
  between operations  6.55 us (2%)
    ppermute x28, waiting for transfers between devices, shards(): arrived = lax.ppermute(moving[c], 'dp', pairs[turns[c]])  112 us
    ppermute x28, waiting for transfers between devices, shards(): moving[c] = lax.ppermute(moving[c], 'dp', pairs[turn])  111 us
    ppermute x28, starting transfers between devices, shards(): arrived = lax.ppermute(moving[c], 'dp', pairs[turns[c]])  30.7 us
    ppermute x28, starting transfers between devices, shards(): moving[c] = lax.ppermute(moving[c], 'dp', pairs[turn])  29.7 us
    dot_general x32, matrix products, contract_tokens(): lax.dot_general(left, right, (((0,), (0,)), ((), ())), preferred_element_...  23.4 us
  transfers between devices with their start and end apart: 58, of which 47 were waited for; matrix products, arithmetic and copies ran while one was open for 11% of the time, Pallas kernels for 0%

profile of v2, /device:TPU:0, one launch (start us, length us, event | category | flops | bytes accessed | tf_op | source)
XLA Modules:
  0.0 356.0 jit_solution(17492029825449198743)
XLA Ops:
  28.6 9.2 %collective-permute-done.5 = bf16[512,512]{1,0:T(8,128)(2,1)S(1)} collective-permute-done((bf16[512,512]{1,0:T(8,128)(2,1)S(1)}, bf16[512,512]{1,0:T(8,128)(2,1)S(1)}, u32[]{:S(2)}, u32[]{:S(2)}) %collective-permute-start.5) | collective-permute-done | bytes 524320 | tf_op jit(solution)/shard_map/ppermute | solution.py:108
  41.1 6.1 %collective-permute-done.3 = bf16[512,512]{1,0:T(8,128)(2,1)S(1)} collective-permute-done((bf16[512,512]{1,0:T(8,128)(2,1)S(1)}, bf16[512,512]{1,0:T(8,128)(2,1)S(1)}, u32[]{:S(2)}, u32[]{:S(2)}) %collective-permute-start.3) | collective-permute-done | bytes 524320 | tf_op jit(solution)/shard_map/ppermute | solution.py:108
  57.0 9.3 %collective-permute-done.8 = bf16[512,512]{1,0:T(8,128)(2,1)S(1)} collective-permute-done((bf16[512,512]{1,0:T(8,128)(2,1)S(1)}, bf16[512,512]{1,0:T(8,128)(2,1)S(1)}, u32[]{:S(2)}, u32[]{:S(2)}) %collective-permute-start.8) | collective-permute-done | bytes 524320 | tf_op jit(solution)/shard_map/ppermute | solution.py:108
  68.4 6.2 %collective-permute-done.9 = bf16[512,512]{1,0:T(8,128)(2,1)S(1)} collective-permute-done((bf16[512,512]{1,0:T(8,128)(2,1)S(1)}, bf16[512,512]{1,0:T(8,128)(2,1)S(1)}, u32[]{:S(2)}, u32[]{:S(2)}) %collective-permute-start.9) | collective-permute-done | bytes 524320 | tf_op jit(solution)/shard_map/ppermute | solution.py:108
  82.4 9.3 %collective-permute-done.13 = bf16[512,512]{1,0:T(8,128)(2,1)S(1)} collective-permute-done((bf16[512,512]{1,0:T(8,128)(2,1)S(1)}, bf16[512,512]{1,0:T(8,128)(2,1)S(1)}, u32[]{:S(2)}, u32[]{:S(2)}) %collective-permute-start.13) | collective-permute-done | bytes 524320 | tf_op jit(solution)/shard_map/ppermute | solution.py:108
  93.5 5.3 %collective-permute-done.11 = bf16[512,512]{1,0:T(8,128)(2,1)S(1)} collective-permute-done((bf16[512,512]{1,0:T(8,128)(2,1)S(1)}, bf16[512,512]{1,0:T(8,128)(2,1)S(1)}, u32[]{:S(2)}, u32[]{:S(2)}) %collective-permute-start.11) | collective-permute-done | bytes 524320 | tf_op jit(solution)/shard_map/ppermute | solution.py:108
  107.4 9.3 %collective-permute-done.17 = bf16[512,512]{1,0:T(8,128)(2,1)S(1)} collective-permute-done((bf16[512,512]{1,0:T(8,128)(2,1)S(1)}, bf16[512,512]{1,0:T(8,128)(2,1)S(1)}, u32[]{:S(2)}, u32[]{:S(2)}) %collective-permute-start.17) | collective-permute-done | bytes 524320 | tf_op jit(solution)/shard_map/ppermute | solution.py:108
  131.6 8.7 %collective-permute-done.21 = bf16[512,512]{1,0:T(8,128)(2,1)S(1)} collective-permute-done((bf16[512,512]{1,0:T(8,128)(2,1)S(1)}, bf16[512,512]{1,0:T(8,128)(2,1)S(1)}, u32[]{:S(2)}, u32[]{:S(2)}) %collective-permute-start.21) | collective-permute-done | bytes 524320 | tf_op jit(solution)/shard_map/ppermute | solution.py:108
  155.7 9.3 %collective-permute-done.23 = bf16[512,512]{1,0:T(8,128)(2,1)S(1)} collective-permute-done((bf16[512,512]{1,0:T(8,128)(2,1)S(1)}, bf16[512,512]{1,0:T(8,128)(2,1)S(1)}, u32[]{:S(2)}, u32[]{:S(2)}) %collective-permute-start.23) | collective-permute-done | bytes 524320 | tf_op jit(solution)/shard_map/ppermute | solution.py:108
  169.4 6.9 %collective-permute-done.26 = bf16[512,512]{1,0:T(8,128)(2,1)S(1)} collective-permute-done((bf16[512,512]{1,0:T(8,128)(2,1)S(1)}, bf16[512,512]{1,0:T(8,128)(2,1)S(1)}, u32[]{:S(2)}, u32[]{:S(2)}) %collective-permute-start.26) | collective-permute-done | bytes 524320 | tf_op jit(solution)/shard_map/ppermute | solution.py:108
  187.9 5.4 %collective-permute-done.27 = bf16[512,512]{1,0:T(8,128)(2,1)S(1)} collective-permute-done((bf16[512,512]{1,0:T(8,128)(2,1)S(1)}, bf16[512,512]{1,0:T(8,128)(2,1)S(1)}, u32[]{:S(2)}, u32[]{:S(2)}) %collective-permute-start.27) | collective-permute-done | bytes 524320 | tf_op jit(solution)/shard_map/ppermute | solution.py:108
  202.3 7.4 %collective-permute-done.33 = bf16[512,512]{1,0:T(8,128)(2,1)} collective-permute-done((bf16[512,512]{1,0:T(8,128)(2,1)S(1)}, bf16[512,512]{1,0:T(8,128)(2,1)}, u32[]{:S(2)}, u32[]{:S(2)}) %collective-permute-start.33) | collective-permute-done | bytes 524320 | tf_op jit(solution)/shard_map/ppermute | solution.py:155
  213.9 6.9 %collective-permute-done.31 = bf16[512,512]{1,0:T(8,128)(2,1)S(1)} collective-permute-done((bf16[512,512]{1,0:T(8,128)(2,1)S(1)}, bf16[512,512]{1,0:T(8,128)(2,1)S(1)}, u32[]{:S(2)}, u32[]{:S(2)}) %collective-permute-start.31) | collective-permute-done | bytes 524320 | tf_op jit(solution)/shard_map/ppermute | solution.py:155
  224.1 6.0 %collective-permute-done.37 = bf16[512,512]{1,0:T(8,128)(2,1)S(1)} collective-permute-done((bf16[512,512]{1,0:T(8,128)(2,1)}, bf16[512,512]{1,0:T(8,128)(2,1)S(1)}, u32[]{:S(2)}, u32[]{:S(2)}) %collective-permute-start.37) | collective-permute-done | bytes 524320 | tf_op jit(solution)/shard_map/ppermute | solution.py:155
  231.9 8.4 %collective-permute-done.35 = bf16[512,512]{1,0:T(8,128)(2,1)S(1)} collective-permute-done((bf16[512,512]{1,0:T(8,128)(2,1)S(1)}, bf16[512,512]{1,0:T(8,128)(2,1)S(1)}, u32[]{:S(2)}, u32[]{:S(2)}) %collective-permute-start.35) | collective-permute-done | bytes 524320 | tf_op jit(solution)/shard_map/ppermute | solution.py:155
  250.2 7.1 %collective-permute-done.41 = bf16[512,512]{1,0:T(8,128)(2,1)} collective-permute-done((bf16[512,512]{1,0:T(8,128)(2,1)S(1)}, bf16[512,512]{1,0:T(8,128)(2,1)}, u32[]{:S(2)}, u32[]{:S(2)}) %collective-permute-start.41) | collective-permute-done | bytes 524320 | tf_op jit(solution)/shard_map/ppermute | solution.py:155
  260.6 8.0 %collective-permute-done.39 = bf16[512,512]{1,0:T(8,128)(2,1)} collective-permute-done((bf16[512,512]{1,0:T(8,128)(2,1)S(1)}, bf16[512,512]{1,0:T(8,128)(2,1)}, u32[]{:S(2)}, u32[]{:S(2)}) %collective-permute-start.39) | collective-permute-done | bytes 524320 | tf_op jit(solution)/shard_map/ppermute | solution.py:155
  272.9 6.8 %collective-permute-done.45 = bf16[512,512]{1,0:T(8,128)(2,1)S(1)} collective-permute-done((bf16[512,512]{1,0:T(8,128)(2,1)}, bf16[512,512]{1,0:T(8,128)(2,1)S(1)}, u32[]{:S(2)}, u32[]{:S(2)}) %collective-permute-start.45) | collective-permute-done | bytes 524320 | tf_op jit(solution)/shard_map/ppermute | solution.py:155
  283.0 8.0 %collective-permute-done.43 = bf16[512,512]{1,0:T(8,128)(2,1)S(1)} collective-permute-done((bf16[512,512]{1,0:T(8,128)(2,1)}, bf16[512,512]{1,0:T(8,128)(2,1)S(1)}, u32[]{:S(2)}, u32[]{:S(2)}) %collective-permute-start.43) | collective-permute-done | bytes 524320 | tf_op jit(solution)/shard_map/ppermute | solution.py:155
  293.2 9.0 %collective-permute-done.49 = bf16[512,512]{1,0:T(8,128)(2,1)S(1)} collective-permute-done((bf16[512,512]{1,0:T(8,128)(2,1)S(1)}, bf16[512,512]{1,0:T(8,128)(2,1)S(1)}, u32[]{:S(2)}, u32[]{:S(2)}) %collective-permute-start.49) | collective-permute-done | bytes 524320 | tf_op jit(solution)/shard_map/ppermute | solution.py:155
  304.4 9.0 %collective-permute-done.47 = bf16[512,512]{1,0:T(8,128)(2,1)S(1)} collective-permute-done((bf16[512,512]{1,0:T(8,128)(2,1)S(1)}, bf16[512,512]{1,0:T(8,128)(2,1)S(1)}, u32[]{:S(2)}, u32[]{:S(2)}) %collective-permute-start.47) | collective-permute-done | bytes 524320 | tf_op jit(solution)/shard_map/ppermute | solution.py:155
  315.7 9.0 %collective-permute-done.53 = bf16[512,512]{1,0:T(8,128)(2,1)S(1)} collective-permute-done((bf16[512,512]{1,0:T(8,128)(2,1)S(1)}, bf16[512,512]{1,0:T(8,128)(2,1)S(1)}, u32[]{:S(2)}, u32[]{:S(2)}) %collective-permute-start.53) | collective-permute-done | bytes 524320 | tf_op jit(solution)/shard_map/ppermute | solution.py:155
  326.9 9.0 %collective-permute-done.51 = bf16[512,512]{1,0:T(8,128)(2,1)S(1)} collective-permute-done((bf16[512,512]{1,0:T(8,128)(2,1)S(1)}, bf16[512,512]{1,0:T(8,128)(2,1)S(1)}, u32[]{:S(2)}, u32[]{:S(2)}) %collective-permute-start.51) | collective-permute-done | bytes 524320 | tf_op jit(solution)/shard_map/ppermute | solution.py:155
  349.9 6.2 %copy-done = bf16[4096,2048]{1,0:T(8,128)(2,1)} copy-done((bf16[4096,2048]{1,0:T(8,128)(2,1)}, bf16[4096,2048]{1,0:T(8,128)(2,1)S(1)}, u32[]{:S(2)}) %copy-start) | copy-done | bytes 16777240
  (225 shorter events, 163.4 us)
Async XLA Ops:
  25.8 21.5 %collective-permute-start.3 = (bf16[512,512]{1,0:T(8,128)(2,1)S(1)}, bf16[512,512]{1,0:T(8,128)(2,1)S(1)}, u32[]{:S(2)}, u32[]{:S(2)}) collective-permute-start(bf16[512,512]{1,0:T(8,128)(2,1)S(1)} %convolution_convert_fusion.30), channel_id=1, source_target_pairs={{0,8},{8,16},{16,24},{24,28},{28,20},{20,12},{12,4},{4,0},{1,9},{9... | collective-permute-start | bytes 1572872 | tf_op jit(solution)/shard_map/ppermute | solution.py:108
  27.8 22.0 %collective-permute-start.2 = (bf16[512,512]{1,0:T(8,128)(2,1)S(1)}, bf16[512,512]{1,0:T(8,128)(2,1)S(1)}, u32[]{:S(2)}, u32[]{:S(2)}) collective-permute-start(bf16[512,512]{1,0:T(8,128)(2,1)S(1)} %convolution_convert_fusion.31), channel_id=1, source_target_pairs={{0,4},{8,0},{16,8},{24,16},{28,24},{20,28},{12,20},{4,12},{1,5},{9... | collective-permute-start | bytes 1572872 | tf_op jit(solution)/shard_map/ppermute | solution.py:108
  53.6 21.1 %collective-permute-start.9 = (bf16[512,512]{1,0:T(8,128)(2,1)S(1)}, bf16[512,512]{1,0:T(8,128)(2,1)S(1)}, u32[]{:S(2)}, u32[]{:S(2)}) collective-permute-start(bf16[512,512]{1,0:T(8,128)(2,1)S(1)} %add_convert_fusion.21), channel_id=1, source_target_pairs={{0,8},{8,16},{16,24},{24,28},{28,20},{20,12},{12,4},{4,0},{1,9},{9... | collective-permute-start | bytes 1572872 | tf_op jit(solution)/shard_map/ppermute | solution.py:108
  55.1 20.8 %collective-permute-start.6 = (bf16[512,512]{1,0:T(8,128)(2,1)S(1)}, bf16[512,512]{1,0:T(8,128)(2,1)S(1)}, u32[]{:S(2)}, u32[]{:S(2)}) collective-permute-start(bf16[512,512]{1,0:T(8,128)(2,1)S(1)} %add_convert_fusion.20), channel_id=1, source_target_pairs={{0,4},{8,0},{16,8},{24,16},{28,24},{20,28},{12,20},{4,12},{1,5},{9... | collective-permute-start | bytes 1572872 | tf_op jit(solution)/shard_map/ppermute | solution.py:108
  78.9 19.9 %collective-permute-start.11 = (bf16[512,512]{1,0:T(8,128)(2,1)S(1)}, bf16[512,512]{1,0:T(8,128)(2,1)S(1)}, u32[]{:S(2)}, u32[]{:S(2)}) collective-permute-start(bf16[512,512]{1,0:T(8,128)(2,1)S(1)} %add_convert_fusion.17), channel_id=1, source_target_pairs={{0,8},{8,16},{16,24},{24,28},{28,20},{20,12},{12,4},{4,0},{1,9},{9... | collective-permute-start | bytes 1572872 | tf_op jit(solution)/shard_map/ppermute | solution.py:108
  152.2 24.1 %collective-permute-start.26 = (bf16[512,512]{1,0:T(8,128)(2,1)S(1)}, bf16[512,512]{1,0:T(8,128)(2,1)S(1)}, u32[]{:S(2)}, u32[]{:S(2)}) collective-permute-start(bf16[512,512]{1,0:T(8,128)(2,1)S(1)} %add_convert_fusion.5), channel_id=1, source_target_pairs={{0,8},{8,16},{16,24},{24,28},{28,20},{20,12},{12,4},{4,0},{1,9},{9... | collective-permute-start | bytes 1572872 | tf_op jit(solution)/shard_map/ppermute | solution.py:108
  153.3 26.0 %collective-permute-start.22 = (bf16[512,512]{1,0:T(8,128)(2,1)S(1)}, bf16[512,512]{1,0:T(8,128)(2,1)S(1)}, u32[]{:S(2)}, u32[]{:S(2)}) collective-permute-start(bf16[512,512]{1,0:T(8,128)(2,1)S(1)} %add_convert_fusion.4), channel_id=1, source_target_pairs={{0,4},{8,0},{16,8},{24,16},{28,24},{20,28},{12,20},{4,12},{1,5},{9... | collective-permute-start | bytes 1572872 | tf_op jit(solution)/shard_map/ppermute | solution.py:108
  200.1 20.8 %collective-permute-start.31 = (bf16[512,512]{1,0:T(8,128)(2,1)S(1)}, bf16[512,512]{1,0:T(8,128)(2,1)S(1)}, u32[]{:S(2)}, u32[]{:S(2)}) collective-permute-start(bf16[512,512]{1,0:T(8,128)(2,1)S(1)} %get-tuple-element.372), channel_id=1, source_target_pairs={{0,8},{8,16},{16,24},{24,28},{28,20},{20,12},{12,4},{4,0},{1,9},{9... | collective-permute-start | bytes 1572872 | tf_op jit(solution)/shard_map/ppermute | solution.py:155
  202.2 21.8 %collective-permute-start.30 = (bf16[512,512]{1,0:T(8,128)(2,1)S(1)}, bf16[512,512]{1,0:T(8,128)(2,1)S(1)}, u32[]{:S(2)}, u32[]{:S(2)}) collective-permute-start(bf16[512,512]{1,0:T(8,128)(2,1)S(1)} %get-tuple-element.371), channel_id=1, source_target_pairs={{0,4},{8,0},{16,8},{24,16},{28,24},{20,28},{12,20},{4,12},{1,5},{9... | collective-permute-start | bytes 1572872 | tf_op jit(solution)/shard_map/ppermute | solution.py:155
  209.7 20.4 %collective-permute-start.37 = (bf16[512,512]{1,0:T(8,128)(2,1)}, bf16[512,512]{1,0:T(8,128)(2,1)S(1)}, u32[]{:S(2)}, u32[]{:S(2)}) collective-permute-start(bf16[512,512]{1,0:T(8,128)(2,1)} %collective-permute-done.33), channel_id=1, source_target_pairs={{0,8},{8,16},{16,24},{24,28},{28,20},{20,12},{12,4},{4,0},{1,9},{9... | collective-permute-start | bytes 1572872 | tf_op jit(solution)/shard_map/ppermute | solution.py:155
  244.4 24.2 %collective-permute-start.39 = (bf16[512,512]{1,0:T(8,128)(2,1)S(1)}, bf16[512,512]{1,0:T(8,128)(2,1)}, u32[]{:S(2)}, u32[]{:S(2)}) collective-permute-start(bf16[512,512]{1,0:T(8,128)(2,1)S(1)} %collective-permute-done.35), channel_id=1, source_target_pairs={{0,8},{8,16},{16,24},{24,28},{28,20},{20,12},{12,4},{4,0},{1,9},{9... | collective-permute-start | bytes 1572872 | tf_op jit(solution)/shard_map/ppermute | solution.py:155
  245.1 25.3 %collective-permute-start.38 = (bf16[512,512]{1,0:T(8,128)(2,1)S(1)}, bf16[512,512]{1,0:T(8,128)(2,1)}, u32[]{:S(2)}, u32[]{:S(2)}) collective-permute-start(bf16[512,512]{1,0:T(8,128)(2,1)S(1)} %collective-permute-done.34), channel_id=1, source_target_pairs={{0,4},{8,0},{16,8},{24,16},{28,24},{20,28},{12,20},{4,12},{1,5},{9... | collective-permute-start | bytes 1572872 | tf_op jit(solution)/shard_map/ppermute | solution.py:155
  257.4 22.4 %collective-permute-start.45 = (bf16[512,512]{1,0:T(8,128)(2,1)}, bf16[512,512]{1,0:T(8,128)(2,1)S(1)}, u32[]{:S(2)}, u32[]{:S(2)}) collective-permute-start(bf16[512,512]{1,0:T(8,128)(2,1)} %collective-permute-done.41), channel_id=1, source_target_pairs={{0,8},{8,16},{16,24},{24,28},{28,20},{20,12},{12,4},{4,0},{1,9},{9... | collective-permute-start | bytes 1572872 | tf_op jit(solution)/shard_map/ppermute | solution.py:155
  258.1 23.4 %collective-permute-start.44 = (bf16[512,512]{1,0:T(8,128)(2,1)}, bf16[512,512]{1,0:T(8,128)(2,1)S(1)}, u32[]{:S(2)}, u32[]{:S(2)}) collective-permute-start(bf16[512,512]{1,0:T(8,128)(2,1)} %collective-permute-done.40), channel_id=1, source_target_pairs={{0,4},{8,0},{16,8},{24,16},{28,24},{20,28},{12,20},{4,12},{1,5},{9... | collective-permute-start | bytes 1572872 | tf_op jit(solution)/shard_map/ppermute | solution.py:155
  268.6 22.4 %collective-permute-start.43 = (bf16[512,512]{1,0:T(8,128)(2,1)}, bf16[512,512]{1,0:T(8,128)(2,1)S(1)}, u32[]{:S(2)}, u32[]{:S(2)}) collective-permute-start(bf16[512,512]{1,0:T(8,128)(2,1)} %collective-permute-done.39), channel_id=1, source_target_pairs={{0,8},{8,16},{16,24},{24,28},{28,20},{20,12},{12,4},{4,0},{1,9},{9... | collective-permute-start | bytes 1572872 | tf_op jit(solution)/shard_map/ppermute | solution.py:155
  270.4 21.3 %collective-permute-start.42 = (bf16[512,512]{1,0:T(8,128)(2,1)}, bf16[512,512]{1,0:T(8,128)(2,1)S(1)}, u32[]{:S(2)}, u32[]{:S(2)}) collective-permute-start(bf16[512,512]{1,0:T(8,128)(2,1)} %collective-permute-done.38), channel_id=1, source_target_pairs={{0,4},{8,0},{16,8},{24,16},{28,24},{20,28},{12,20},{4,12},{1,5},{9... | collective-permute-start | bytes 1572872 | tf_op jit(solution)/shard_map/ppermute | solution.py:155
  279.7 22.5 %collective-permute-start.49 = (bf16[512,512]{1,0:T(8,128)(2,1)S(1)}, bf16[512,512]{1,0:T(8,128)(2,1)S(1)}, u32[]{:S(2)}, u32[]{:S(2)}) collective-permute-start(bf16[512,512]{1,0:T(8,128)(2,1)S(1)} %collective-permute-done.45), channel_id=1, source_target_pairs={{0,8},{8,16},{16,24},{24,28},{28,20},{20,12},{12,4},{4,0},{1,9},{9... | collective-permute-start | bytes 1572872 | tf_op jit(solution)/shard_map/ppermute | solution.py:155
  281.6 21.4 %collective-permute-start.48 = (bf16[512,512]{1,0:T(8,128)(2,1)S(1)}, bf16[512,512]{1,0:T(8,128)(2,1)S(1)}, u32[]{:S(2)}, u32[]{:S(2)}) collective-permute-start(bf16[512,512]{1,0:T(8,128)(2,1)S(1)} %collective-permute-done.44), channel_id=1, source_target_pairs={{0,4},{8,0},{16,8},{24,16},{28,24},{20,28},{12,20},{4,12},{1,5},{9... | collective-permute-start | bytes 1572872 | tf_op jit(solution)/shard_map/ppermute | solution.py:155
  291.0 22.5 %collective-permute-start.47 = (bf16[512,512]{1,0:T(8,128)(2,1)S(1)}, bf16[512,512]{1,0:T(8,128)(2,1)S(1)}, u32[]{:S(2)}, u32[]{:S(2)}) collective-permute-start(bf16[512,512]{1,0:T(8,128)(2,1)S(1)} %collective-permute-done.43), channel_id=1, source_target_pairs={{0,8},{8,16},{16,24},{24,28},{28,20},{20,12},{12,4},{4,0},{1,9},{9... | collective-permute-start | bytes 1572872 | tf_op jit(solution)/shard_map/ppermute | solution.py:155
  291.7 22.5 %collective-permute-start.46 = (bf16[512,512]{1,0:T(8,128)(2,1)S(1)}, bf16[512,512]{1,0:T(8,128)(2,1)S(1)}, u32[]{:S(2)}, u32[]{:S(2)}) collective-permute-start(bf16[512,512]{1,0:T(8,128)(2,1)S(1)} %collective-permute-done.42), channel_id=1, source_target_pairs={{0,4},{8,0},{16,8},{24,16},{28,24},{20,28},{12,20},{4,12},{1,5},{9... | collective-permute-start | bytes 1572872 | tf_op jit(solution)/shard_map/ppermute | solution.py:155
  302.2 22.5 %collective-permute-start.53 = (bf16[512,512]{1,0:T(8,128)(2,1)S(1)}, bf16[512,512]{1,0:T(8,128)(2,1)S(1)}, u32[]{:S(2)}, u32[]{:S(2)}) collective-permute-start(bf16[512,512]{1,0:T(8,128)(2,1)S(1)} %collective-permute-done.49), channel_id=1, source_target_pairs={{0,8},{8,16},{16,24},{24,28},{28,20},{20,12},{12,4},{4,0},{1,9},{9... | collective-permute-start | bytes 1572872 | tf_op jit(solution)/shard_map/ppermute | solution.py:155
  303.0 22.5 %collective-permute-start.52 = (bf16[512,512]{1,0:T(8,128)(2,1)S(1)}, bf16[512,512]{1,0:T(8,128)(2,1)S(1)}, u32[]{:S(2)}, u32[]{:S(2)}) collective-permute-start(bf16[512,512]{1,0:T(8,128)(2,1)S(1)} %collective-permute-done.48), channel_id=1, source_target_pairs={{0,4},{8,0},{16,8},{24,16},{28,24},{20,28},{12,20},{4,12},{1,5},{9... | collective-permute-start | bytes 1572872 | tf_op jit(solution)/shard_map/ppermute | solution.py:155
  313.4 22.5 %collective-permute-start.51 = (bf16[512,512]{1,0:T(8,128)(2,1)S(1)}, bf16[512,512]{1,0:T(8,128)(2,1)S(1)}, u32[]{:S(2)}, u32[]{:S(2)}) collective-permute-start(bf16[512,512]{1,0:T(8,128)(2,1)S(1)} %collective-permute-done.47), channel_id=1, source_target_pairs={{0,8},{8,16},{16,24},{24,28},{28,20},{20,12},{12,4},{4,0},{1,9},{9... | collective-permute-start | bytes 1572872 | tf_op jit(solution)/shard_map/ppermute | solution.py:155
  314.2 22.5 %collective-permute-start.50 = (bf16[512,512]{1,0:T(8,128)(2,1)S(1)}, bf16[512,512]{1,0:T(8,128)(2,1)S(1)}, u32[]{:S(2)}, u32[]{:S(2)}) collective-permute-start(bf16[512,512]{1,0:T(8,128)(2,1)S(1)} %collective-permute-done.46), channel_id=1, source_target_pairs={{0,4},{8,0},{16,8},{24,16},{28,24},{20,28},{12,20},{4,12},{1,5},{9... | collective-permute-start | bytes 1572872 | tf_op jit(solution)/shard_map/ppermute | solution.py:155
  (41 other events, 579.4 us)

commit v3 on v2

--- a/solution.py
+++ b/solution.py
@@ -3,6 +3,8 @@
 import jax
 import jax.numpy as jnp
 from jax import lax
+from jax.experimental import pallas as pl
+from jax.experimental.pallas import tpu as pltpu
 from jax.experimental.layout import Layout, with_layout_constraint
 from jax.sharding import PartitionSpec as P
 
@@ -10,6 +12,9 @@
 OUTER = 4
 CHUNKS = 4
 LAG = 2
+HOIST = 28
+SPREAD = (1, 2, 3, 4)
+FREE = 1
 AHEAD = 3
 
 
@@ -47,6 +52,37 @@
     return with_layout_constraint(value, Layout(major_to_minor=(0, 1)))
 
 
+def place(whole, piece, row, column):
+    shape, in_place = whole.shape, not isinstance(whole, jax.ShapeDtypeStruct)
+
+    def body(row_ref, piece_ref, *rest):
+        whole_ref, sem = rest[-2:]
+        first = pl.multiple_of(row_ref[0], piece.shape[0])
+        copy = pltpu.make_async_copy(
+            piece_ref,
+            whole_ref.at[pl.ds(first, piece.shape[0]), pl.ds(column, piece.shape[1])],
+            sem,
+        )
+        copy.start()
+        copy.wait()
+
+    return pl.pallas_call(
+        body,
+        out_shape=jax.ShapeDtypeStruct(shape, whole.dtype),
+        grid_spec=pltpu.PrefetchScalarGridSpec(
+            num_scalar_prefetch=1,
+            grid=(1,),
+            in_specs=[pl.BlockSpec(memory_space=pl.ANY)]
+            + [pl.BlockSpec(memory_space=pltpu.HBM)] * in_place,
+            out_specs=pl.BlockSpec(memory_space=pltpu.HBM),
+            scratch_shapes=[pltpu.SemaphoreType.DMA],
+        ),
+        input_output_aliases={2: 0} if in_place else {},
+        compiler_params=pltpu.CompilerParams(vmem_limit_bytes=1 << 20),
+        cost_estimate=pl.CostEstimate(flops=0, bytes_accessed=1024, transcendentals=0),
+    )(row.reshape(1), piece, *([whole] if in_place else []))
+
+
 def cycle(count):
     inner = count // OUTER
     walk = [o * inner for o in range(OUTER)]
@@ -60,10 +96,10 @@
     count = lax.psum(1, "dp")
     rows, wide = master.shape
     walk = cycle(count)
-    place = [walk.index(d) for d in range(count)]
+    places = [walk.index(d) for d in range(count)]
     me = lax.axis_index("dp")
     table = jnp.asarray(
-        [[walk[(place[d] + k) % count] for k in range(count)] for d in range(count)], jnp.int32
+        [[walk[(places[d] + k) % count] for k in range(count)] for d in range(count)], jnp.int32
     )[me]
     owners = [table[k] for k in range(count)]
     pairs = {
@@ -108,51 +144,59 @@
         arrived = lax.ppermute(moving[c], "dp", pairs[turns[c]])
         if number == 0:
             gate = prepare(0, gate)
-        arrived, gate = lax.optimization_barrier((arrived, gate))
+        if number < FREE:
+            arrived, gate = lax.optimization_barrier((arrived, gate))
         if number == 0:
-            for early in range(1, AHEAD):
+            for early in range(1, HOIST):
                 gate = prepare(early, gate)
         moving[c] = arrived.astype(jnp.float32) + terms.pop(number).astype(jnp.float32)
         if step < count - 1:
             moving[c] = straight(moving[c].astype(jnp.bfloat16))
-        moving[c], gate = lax.optimization_barrier((moving[c], gate))
-        gate = prepare(number + AHEAD, gate)
-    new_weights = jnp.zeros((count * rows, wide), jnp.bfloat16)
+        if number < FREE:
+            moving[c], gate = lax.optimization_barrier((moving[c], gate))
+        while len(terms) + number + 1 < min(max(HOIST, number + 1 + AHEAD), len(events)):
+            gate = prepare(len(terms) + number + 1, gate)
+    new_weights = jax.ShapeDtypeStruct((count * rows, wide), jnp.bfloat16)
+    new_one = new_two = jax.ShapeDtypeStruct((rows, wide), jnp.float32)
+    top = jnp.zeros((), jnp.int32)
     ones, twos = [], []
     for c in range(CHUNKS):
         grad = moving[c]
         if c:
             grad, moving[c - 1] = lax.optimization_barrier((grad, moving[c - 1]))
-        new_one = beta_one * moment_one[:, cols[c]] + (1.0 - beta_one) * grad
-        new_two = beta_two * moment_two[:, cols[c]] + (1.0 - beta_two) * grad * grad
-        first = new_one / (1.0 - beta_one**adam_step)
-        second = new_two / (1.0 - beta_two**adam_step)
+        one = beta_one * moment_one[:, cols[c]] + (1.0 - beta_one) * grad
+        two = beta_two * moment_two[:, cols[c]] + (1.0 - beta_two) * grad * grad
+        first = one / (1.0 - beta_one**adam_step)
+        second = two / (1.0 - beta_two**adam_step)
         update = learn_rate * (
             first / (jnp.sqrt(second) + epsilon) + weight_decay * master[:, cols[c]]
         )
         moving[c] = straight((master[:, cols[c]] - update).astype(jnp.bfloat16))
-        ones.append(new_one)
-        twos.append(new_two)
-    new_one, new_two = jnp.concatenate(ones, axis=1), jnp.concatenate(twos, axis=1)
+        ones.append(straight(one))
+        twos.append(straight(two))
     waiting = collections.deque()
 
     def put(into):
         c, step, piece = waiting.popleft()
         at = owners[-turns[c] * step % count]
-        return lax.dynamic_update_slice(into, piece, (at * rows, c * part))
+        return place(into, piece, at * rows, c * part)
 
     for step in range(count):
-        if step == 3:
-            new_weights, new_one, new_two = lax.optimization_barrier(
-                (new_weights, new_one, new_two)
-            )
         for c, turn in enumerate(turns):
             waiting.append((c, step, moving[c]))
             if len(waiting) > LAG:
                 new_weights = put(new_weights)
             if step < count - 1:
-                moving[c], new_weights = lax.optimization_barrier((moving[c], new_weights))
+                if step or c >= LAG:
+                    moving[c], new_weights = lax.optimization_barrier((moving[c], new_weights))
                 moving[c] = lax.ppermute(moving[c], "dp", pairs[turn])
+        for c in range(CHUNKS):
+            if SPREAD[c] == step:
+                new_one = place(new_one, ones[c], top, c * part)
+                new_two = place(new_two, twos[c], top, c * part)
+                new_weights, new_one, new_two = lax.optimization_barrier(
+                    (new_weights, new_one, new_two)
+                )
     while waiting:
         new_weights = put(new_weights)
     return (new_weights, new_one, new_two)

time: 357 us -> 344 us (0.964)
  waiting for transfers between devices: 224 us -> 176 us
  Pallas kernels: 0 us -> 33.5 us
  starting transfers between devices: 66.6 us -> 87.7 us
  local copies, waits for them, and re-layouts: 17.7 us -> 2.44 us
  other arithmetic: 17.2 us -> 12.9 us
    pallas_call x0 -> x40, Pallas kernels: none -> 33.5 us  [place(): pl.pallas_call(body, out_shape=jax.ShapeDtypeStruct(shape, whole.dtype),...]
    ppermute x28, waiting for transfers between devices: 111 us -> 80.8 us  [shards(): moving[c] = lax.ppermute(moving[c], 'dp', pairs[turn])]
    ppermute x28, waiting for transfers between devices: 112 us -> 95.3 us  [shards(): arrived = lax.ppermute(moving[c], 'dp', pairs[turns[c]])]
    ppermute x28, starting transfers between devices: 29.7 us -> 43 us  [shards(): moving[c] = lax.ppermute(moving[c], 'dp', pairs[turn])]
    ppermute x28, starting transfers between devices: 30.7 us -> 38.6 us  [shards(): arrived = lax.ppermute(moving[c], 'dp', pairs[turns[c]])]
    dynamic_update_slice x32 -> x0, local copies, waits for them, and re-layouts: 7.06 us -> none  [put(): return lax.dynamic_update_slice(into, piece, (at * rows, c * part))]
    unnamed x14 -> x12, local copies, waits for them, and re-layouts: 6.19 us -> 0.03 us
    concatenate x1 -> x0, other arithmetic: 3.7 us -> none  [shards(): jnp.concatenate(ones, axis=1)]
  transfers between devices with their start and end apart: 58 -> 58, of which waited for: 47 -> 50; matrix products, arithmetic and copies ran while one was open for 11% -> 10% of each run, Pallas kernels for 0% -> 10%
where the time goes in v3:
time: 344 us
  waiting for transfers between devices  176 us (51%)
  starting transfers between devices  87.7 us (25%)
  Pallas kernels  33.5 us (10%)
  matrix products  24.4 us (7%)
  other arithmetic  12.9 us (4%)
  between operations  6.65 us (2%)
    ppermute x28, waiting for transfers between devices, shards(): arrived = lax.ppermute(moving[c], 'dp', pairs[turns[c]])  95.3 us
    ppermute x28, waiting for transfers between devices, shards(): moving[c] = lax.ppermute(moving[c], 'dp', pairs[turn])  80.8 us
    ppermute x28, starting transfers between devices, shards(): moving[c] = lax.ppermute(moving[c], 'dp', pairs[turn])  43 us
    ppermute x28, starting transfers between devices, shards(): arrived = lax.ppermute(moving[c], 'dp', pairs[turns[c]])  38.6 us
    pallas_call x40, Pallas kernels, place(): pl.pallas_call(body, out_shape=jax.ShapeDtypeStruct(shape, whole.dtype),...  33.5 us
    dot_general x32, matrix products, contract_tokens(): lax.dot_general(left, right, (((0,), (0,)), ((), ())), preferred_element_...  23.4 us
  transfers between devices with their start and end apart: 58, of which 50 were waited for; matrix products, arithmetic and copies ran while one was open for 10% of the time, Pallas kernels for 10%

profile of v3, /device:TPU:0, one launch (start us, length us, event | category | flops | bytes accessed | tf_op | source)
XLA Modules:
  0.0 343.7 jit_solution(15101891143239152083)
XLA Ops:
  1.4 4.8 %collective-permute-start = (f32[64]{0:T(128)S(1)}, f32[64]{0:T(128)S(1)}, u32[]{:S(2)}, u32[]{:S(2)}) collective-permute-start(f32[64]{0:T(128)S(1)} %convert_reduce_fusion), channel_id=1, source_target_pairs={{0,4},{4,8},{8,12},{12,16},{16,20},{20,24},{24,28},{1,5},{5,9},{9,... | collective-permute-start | bytes 776 | tf_op jit(solution)/shard_map/ppermute | solution.py:35
  21.6 3.7 %collective-permute-start.3 = (bf16[512,512]{1,0:T(8,128)(2,1)S(1)}, bf16[512,512]{1,0:T(8,128)(2,1)S(1)}, u32[]{:S(2)}, u32[]{:S(2)}) collective-permute-start(bf16[512,512]{1,0:T(8,128)(2,1)S(1)} %convolution_convert_fusion.28), channel_id=1, source_target_pairs={{0,8},{8,16},{16,24},{24,28},{28,20},{20,12},{12,4},{4,0},{1,9},{9... | collective-permute-start | bytes 1572872 | tf_op jit(solution)/shard_map/ppermute | solution.py:144
  28.5 9.2 %collective-permute-done.3 = bf16[512,512]{1,0:T(8,128)(2,1)S(1)} collective-permute-done((bf16[512,512]{1,0:T(8,128)(2,1)S(1)}, bf16[512,512]{1,0:T(8,128)(2,1)S(1)}, u32[]{:S(2)}, u32[]{:S(2)}) %collective-permute-start.3) | collective-permute-done | bytes 524320 | tf_op jit(solution)/shard_map/ppermute | solution.py:144
  66.5 6.6 %collective-permute-done.11 = bf16[512,512]{1,0:T(8,128)(2,1)S(1)} collective-permute-done((bf16[512,512]{1,0:T(8,128)(2,1)S(1)}, bf16[512,512]{1,0:T(8,128)(2,1)S(1)}, u32[]{:S(2)}, u32[]{:S(2)}) %collective-permute-start.11) | collective-permute-done | bytes 524320 | tf_op jit(solution)/shard_map/ppermute | solution.py:144
  77.3 7.0 %collective-permute-done.25 = bf16[512,512]{1,0:T(8,128)(2,1)S(1)} collective-permute-done((bf16[512,512]{1,0:T(8,128)(2,1)S(1)}, bf16[512,512]{1,0:T(8,128)(2,1)S(1)}, u32[]{:S(2)}, u32[]{:S(2)}) %collective-permute-start.25) | collective-permute-done | bytes 524320 | tf_op jit(solution)/shard_map/ppermute | solution.py:144
  88.5 7.0 %collective-permute-done.12 = bf16[512,512]{1,0:T(8,128)(2,1)S(1)} collective-permute-done((bf16[512,512]{1,0:T(8,128)(2,1)S(1)}, bf16[512,512]{1,0:T(8,128)(2,1)S(1)}, u32[]{:S(2)}, u32[]{:S(2)}) %collective-permute-start.12) | collective-permute-done | bytes 524320 | tf_op jit(solution)/shard_map/ppermute | solution.py:144
  99.8 7.0 %collective-permute-done.26 = bf16[512,512]{1,0:T(8,128)(2,1)S(1)} collective-permute-done((bf16[512,512]{1,0:T(8,128)(2,1)S(1)}, bf16[512,512]{1,0:T(8,128)(2,1)S(1)}, u32[]{:S(2)}, u32[]{:S(2)}) %collective-permute-start.26) | collective-permute-done | bytes 524320 | tf_op jit(solution)/shard_map/ppermute | solution.py:144
  111.0 7.0 %collective-permute-done.13 = bf16[512,512]{1,0:T(8,128)(2,1)S(1)} collective-permute-done((bf16[512,512]{1,0:T(8,128)(2,1)S(1)}, bf16[512,512]{1,0:T(8,128)(2,1)S(1)}, u32[]{:S(2)}, u32[]{:S(2)}) %collective-permute-start.13) | collective-permute-done | bytes 524320 | tf_op jit(solution)/shard_map/ppermute | solution.py:144
  122.2 7.0 %collective-permute-done.27 = bf16[512,512]{1,0:T(8,128)(2,1)S(1)} collective-permute-done((bf16[512,512]{1,0:T(8,128)(2,1)S(1)}, bf16[512,512]{1,0:T(8,128)(2,1)S(1)}, u32[]{:S(2)}, u32[]{:S(2)}) %collective-permute-start.27) | collective-permute-done | bytes 524320 | tf_op jit(solution)/shard_map/ppermute | solution.py:144
  133.4 7.0 %collective-permute-done.14 = bf16[512,512]{1,0:T(8,128)(2,1)S(1)} collective-permute-done((bf16[512,512]{1,0:T(8,128)(2,1)S(1)}, bf16[512,512]{1,0:T(8,128)(2,1)S(1)}, u32[]{:S(2)}, u32[]{:S(2)}) %collective-permute-start.14) | collective-permute-done | bytes 524320 | tf_op jit(solution)/shard_map/ppermute | solution.py:144
  144.7 6.9 %collective-permute-done.28 = bf16[512,512]{1,0:T(8,128)(2,1)S(1)} collective-permute-done((bf16[512,512]{1,0:T(8,128)(2,1)S(1)}, bf16[512,512]{1,0:T(8,128)(2,1)S(1)}, u32[]{:S(2)}, u32[]{:S(2)}) %collective-permute-start.28) | collective-permute-done | bytes 524320 | tf_op jit(solution)/shard_map/ppermute | solution.py:144
  155.9 7.0 %collective-permute-done.15 = bf16[512,512]{1,0:T(8,128)(2,1)S(1)} collective-permute-done((bf16[512,512]{1,0:T(8,128)(2,1)S(1)}, bf16[512,512]{1,0:T(8,128)(2,1)S(1)}, u32[]{:S(2)}, u32[]{:S(2)}) %collective-permute-start.15) | collective-permute-done | bytes 524320 | tf_op jit(solution)/shard_map/ppermute | solution.py:144
  167.2 7.0 %collective-permute-done.29 = bf16[512,512]{1,0:T(8,128)(2,1)S(1)} collective-permute-done((bf16[512,512]{1,0:T(8,128)(2,1)S(1)}, bf16[512,512]{1,0:T(8,128)(2,1)S(1)}, u32[]{:S(2)}, u32[]{:S(2)}) %collective-permute-start.29) | collective-permute-done | bytes 524320 | tf_op jit(solution)/shard_map/ppermute | solution.py:144
  180.5 4.8 %collective-permute-done.16 = bf16[512,512]{1,0:T(8,128)(2,1)S(1)} collective-permute-done((bf16[512,512]{1,0:T(8,128)(2,1)S(1)}, bf16[512,512]{1,0:T(8,128)(2,1)S(1)}, u32[]{:S(2)}, u32[]{:S(2)}) %collective-permute-start.16) | collective-permute-done | bytes 524320 | tf_op jit(solution)/shard_map/ppermute | solution.py:144
  193.5 3.1 collective-permute-done.33.piece_ref
  204.6 3.2 collective-permute-done.32.piece_ref
  227.1 3.2 collective-permute-done.36.piece_ref
  249.6 3.2 collective-permute-done.40.piece_ref
  272.0 3.2 collective-permute-done.44.piece_ref
  287.3 5.3 %collective-permute-done.47.piece_ref = bf16[512,512]{1,0:T(8,128)(2,1)S(1)} collective-permute-done((bf16[512,512]{1,0:T(8,128)(2,1)S(1)}, bf16[512,512]{1,0:T(8,128)(2,1)S(1)}, u32[]{:S(2)}, u32[]{:S(2)}) %collective-permute-start.47) | collective-permute-done | bytes 524320 | tf_op jit(solution)/shard_map/ppermute | solution.py:192
  305.7 3.2 collective-permute-done.53.piece_ref
  309.8 4.9 %collective-permute-done.51.piece_ref = bf16[512,512]{1,0:T(8,128)(2,1)S(1)} collective-permute-done((bf16[512,512]{1,0:T(8,128)(2,1)S(1)}, bf16[512,512]{1,0:T(8,128)(2,1)S(1)}, u32[]{:S(2)}, u32[]{:S(2)}) %collective-permute-start.51) | collective-permute-done | bytes 524320 | tf_op jit(solution)/shard_map/ppermute | solution.py:192
  317.6 3.5 %collective-permute-done.50.piece_ref = bf16[512,512]{1,0:T(8,128)(2,1)S(1)} collective-permute-done((bf16[512,512]{1,0:T(8,128)(2,1)S(1)}, bf16[512,512]{1,0:T(8,128)(2,1)S(1)}, u32[]{:S(2)}, u32[]{:S(2)}) %collective-permute-start.50) | collective-permute-done | bytes 524320 | tf_op jit(solution)/shard_map/ppermute | solution.py:192
  326.8 7.1 %collective-permute-done.57.piece_ref = bf16[512,512]{1,0:T(8,128)(2,1)S(1)} collective-permute-done((bf16[512,512]{1,0:T(8,128)(2,1)S(1)}, bf16[512,512]{1,0:T(8,128)(2,1)S(1)}, u32[]{:S(2)}, u32[]{:S(2)}) %collective-permute-start.57) | collective-permute-done | bytes 524320 | tf_op jit(solution)/shard_map/ppermute | solution.py:192
  (224 shorter events, 205.3 us)
Async XLA Ops:
  25.6 25.2 %collective-permute-start.17 = (bf16[512,512]{1,0:T(8,128)(2,1)S(1)}, bf16[512,512]{1,0:T(8,128)(2,1)S(1)}, u32[]{:S(2)}, u32[]{:S(2)}) collective-permute-start(bf16[512,512]{1,0:T(8,128)(2,1)S(1)} %convolution_convert_fusion.29), channel_id=1, source_target_pairs={{0,4},{8,0},{16,8},{24,16},{28,24},{20,28},{12,20},{4,12},{1,5},{9... | collective-permute-start | bytes 1572872 | tf_op jit(solution)/shard_map/ppermute | solution.py:144
  25.7 27.5 %collective-permute-start.10 = (bf16[512,512]{1,0:T(8,128)(2,1)S(1)}, bf16[512,512]{1,0:T(8,128)(2,1)S(1)}, u32[]{:S(2)}, u32[]{:S(2)}) collective-permute-start(bf16[512,512]{1,0:T(8,128)(2,1)S(1)} %convolution_convert_fusion.30), channel_id=1, source_target_pairs={{0,8},{8,16},{16,24},{24,28},{28,20},{20,12},{12,4},{4,0},{1,9},{9... | collective-permute-start | bytes 1572872 | tf_op jit(solution)/shard_map/ppermute | solution.py:144
  27.7 31.2 %collective-permute-start.2 = (bf16[512,512]{1,0:T(8,128)(2,1)S(1)}, bf16[512,512]{1,0:T(8,128)(2,1)S(1)}, u32[]{:S(2)}, u32[]{:S(2)}) collective-permute-start(bf16[512,512]{1,0:T(8,128)(2,1)S(1)} %convolution_convert_fusion.31), channel_id=1, source_target_pairs={{0,4},{8,0},{16,8},{24,16},{28,24},{20,28},{12,20},{4,12},{1,5},{9... | collective-permute-start | bytes 1572872 | tf_op jit(solution)/shard_map/ppermute | solution.py:144
  73.2 22.3 %collective-permute-start.12 = (bf16[512,512]{1,0:T(8,128)(2,1)S(1)}, bf16[512,512]{1,0:T(8,128)(2,1)S(1)}, u32[]{:S(2)}, u32[]{:S(2)}) collective-permute-start(bf16[512,512]{1,0:T(8,128)(2,1)S(1)} %add_convert_fusion.16), channel_id=1, source_target_pairs={{0,8},{8,16},{16,24},{24,28},{28,20},{20,12},{12,4},{4,0},{1,9},{9... | collective-permute-start | bytes 1572872 | tf_op jit(solution)/shard_map/ppermute | solution.py:144
  106.9 22.3 %collective-permute-start.27 = (bf16[512,512]{1,0:T(8,128)(2,1)S(1)}, bf16[512,512]{1,0:T(8,128)(2,1)S(1)}, u32[]{:S(2)}, u32[]{:S(2)}) collective-permute-start(bf16[512,512]{1,0:T(8,128)(2,1)S(1)} %add_convert_fusion.2), channel_id=1, source_target_pairs={{0,8},{8,16},{16,24},{24,28},{28,20},{20,12},{12,4},{4,0},{1,9},{9... | collective-permute-start | bytes 1572872 | tf_op jit(solution)/shard_map/ppermute | solution.py:144
  129.4 22.3 %collective-permute-start.28 = (bf16[512,512]{1,0:T(8,128)(2,1)S(1)}, bf16[512,512]{1,0:T(8,128)(2,1)S(1)}, u32[]{:S(2)}, u32[]{:S(2)}) collective-permute-start(bf16[512,512]{1,0:T(8,128)(2,1)S(1)} %add_convert_fusion.1), channel_id=1, source_target_pairs={{0,8},{8,16},{16,24},{24,28},{28,20},{20,12},{12,4},{4,0},{1,9},{9... | collective-permute-start | bytes 1572872 | tf_op jit(solution)/shard_map/ppermute | solution.py:144
  151.8 22.3 %collective-permute-start.29 = (bf16[512,512]{1,0:T(8,128)(2,1)S(1)}, bf16[512,512]{1,0:T(8,128)(2,1)S(1)}, u32[]{:S(2)}, u32[]{:S(2)}) collective-permute-start(bf16[512,512]{1,0:T(8,128)(2,1)S(1)} %add_convert_fusion), channel_id=1, source_target_pairs={{0,8},{8,16},{16,24},{24,28},{28,20},{20,12},{12,4},{4,0},{1,9},{9... | collective-permute-start | bytes 1572872 | tf_op jit(solution)/shard_map/ppermute | solution.py:144
  191.7 22.3 %collective-permute-start.30 = (bf16[512,512]{1,0:T(8,128)(2,1)S(1)}, bf16[512,512]{1,0:T(8,128)(2,1)S(1)}, u32[]{:S(2)}, u32[]{:S(2)}) collective-permute-start(bf16[512,512]{1,0:T(8,128)(2,1)S(1)} %get-tuple-element.195.piece_ref), channel_id=1, source_target_pairs={{0,4},{8,0},{16,8},{24,16},{28,24},{20,28},{12,20},{4,12},{1,5},{9... | collective-permute-start | bytes 1572872 | tf_op jit(solution)/shard_map/ppermute | solution.py:192
  196.6 22.5 %collective-permute-start.37 = (bf16[512,512]{1,0:T(8,128)(2,1)S(1)}, bf16[512,512]{1,0:T(8,128)(2,1)S(1)}, u32[]{:S(2)}, u32[]{:S(2)}) collective-permute-start(bf16[512,512]{1,0:T(8,128)(2,1)S(1)} %collective-permute-done.33.piece_ref), channel_id=1, source_target_pairs={{0,8},{8,16},{16,24},{24,28},{28,20},{20,12},{12,4},{4,0},{1,9},{9... | collective-permute-start | bytes 1572872 | tf_op jit(solution)/shard_map/ppermute | solution.py:192
  202.8 22.5 %collective-permute-start.35 = (bf16[512,512]{1,0:T(8,128)(2,1)S(1)}, bf16[512,512]{1,0:T(8,128)(2,1)S(1)}, u32[]{:S(2)}, u32[]{:S(2)}) collective-permute-start(bf16[512,512]{1,0:T(8,128)(2,1)S(1)} %collective-permute-done.31.piece_ref), channel_id=1, source_target_pairs={{0,4},{8,0},{16,8},{24,16},{28,24},{20,28},{12,20},{4,12},{1,5},{9... | collective-permute-start | bytes 1572872 | tf_op jit(solution)/shard_map/ppermute | solution.py:192
  207.8 22.5 %collective-permute-start.36 = (bf16[512,512]{1,0:T(8,128)(2,1)S(1)}, bf16[512,512]{1,0:T(8,128)(2,1)S(1)}, u32[]{:S(2)}, u32[]{:S(2)}) collective-permute-start(bf16[512,512]{1,0:T(8,128)(2,1)S(1)} %collective-permute-done.32.piece_ref), channel_id=1, source_target_pairs={{0,8},{8,16},{16,24},{24,28},{28,20},{20,12},{12,4},{4,0},{1,9},{9... | collective-permute-start | bytes 1572872 | tf_op jit(solution)/shard_map/ppermute | solution.py:192
  214.0 22.5 %collective-permute-start.34 = (bf16[512,512]{1,0:T(8,128)(2,1)S(1)}, bf16[512,512]{1,0:T(8,128)(2,1)S(1)}, u32[]{:S(2)}, u32[]{:S(2)}) collective-permute-start(bf16[512,512]{1,0:T(8,128)(2,1)S(1)} %collective-permute-done.30.piece_ref), channel_id=1, source_target_pairs={{0,4},{8,0},{16,8},{24,16},{28,24},{20,28},{12,20},{4,12},{1,5},{9... | collective-permute-start | bytes 1572872 | tf_op jit(solution)/shard_map/ppermute | solution.py:192
  219.1 22.5 %collective-permute-start.41 = (bf16[512,512]{1,0:T(8,128)(2,1)S(1)}, bf16[512,512]{1,0:T(8,128)(2,1)S(1)}, u32[]{:S(2)}, u32[]{:S(2)}) collective-permute-start(bf16[512,512]{1,0:T(8,128)(2,1)S(1)} %collective-permute-done.37.piece_ref), channel_id=1, source_target_pairs={{0,8},{8,16},{16,24},{24,28},{28,20},{20,12},{12,4},{4,0},{1,9},{9... | collective-permute-start | bytes 1572872 | tf_op jit(solution)/shard_map/ppermute | solution.py:192
  225.2 22.5 %collective-permute-start.39 = (bf16[512,512]{1,0:T(8,128)(2,1)S(1)}, bf16[512,512]{1,0:T(8,128)(2,1)S(1)}, u32[]{:S(2)}, u32[]{:S(2)}) collective-permute-start(bf16[512,512]{1,0:T(8,128)(2,1)S(1)} %collective-permute-done.35.piece_ref), channel_id=1, source_target_pairs={{0,4},{8,0},{16,8},{24,16},{28,24},{20,28},{12,20},{4,12},{1,5},{9... | collective-permute-start | bytes 1572872 | tf_op jit(solution)/shard_map/ppermute | solution.py:192
  230.3 22.5 %collective-permute-start.40 = (bf16[512,512]{1,0:T(8,128)(2,1)S(1)}, bf16[512,512]{1,0:T(8,128)(2,1)S(1)}, u32[]{:S(2)}, u32[]{:S(2)}) collective-permute-start(bf16[512,512]{1,0:T(8,128)(2,1)S(1)} %collective-permute-done.36.piece_ref), channel_id=1, source_target_pairs={{0,8},{8,16},{16,24},{24,28},{28,20},{20,12},{12,4},{4,0},{1,9},{9... | collective-permute-start | bytes 1572872 | tf_op jit(solution)/shard_map/ppermute | solution.py:192
  236.5 22.5 %collective-permute-start.38 = (bf16[512,512]{1,0:T(8,128)(2,1)S(1)}, bf16[512,512]{1,0:T(8,128)(2,1)S(1)}, u32[]{:S(2)}, u32[]{:S(2)}) collective-permute-start(bf16[512,512]{1,0:T(8,128)(2,1)S(1)} %collective-permute-done.34.piece_ref), channel_id=1, source_target_pairs={{0,4},{8,0},{16,8},{24,16},{28,24},{20,28},{12,20},{4,12},{1,5},{9... | collective-permute-start | bytes 1572872 | tf_op jit(solution)/shard_map/ppermute | solution.py:192
  241.6 22.5 %collective-permute-start.45 = (bf16[512,512]{1,0:T(8,128)(2,1)S(1)}, bf16[512,512]{1,0:T(8,128)(2,1)S(1)}, u32[]{:S(2)}, u32[]{:S(2)}) collective-permute-start(bf16[512,512]{1,0:T(8,128)(2,1)S(1)} %collective-permute-done.41.piece_ref), channel_id=1, source_target_pairs={{0,8},{8,16},{16,24},{24,28},{28,20},{20,12},{12,4},{4,0},{1,9},{9... | collective-permute-start | bytes 1572872 | tf_op jit(solution)/shard_map/ppermute | solution.py:192
  247.7 22.5 %collective-permute-start.43 = (bf16[512,512]{1,0:T(8,128)(2,1)S(1)}, bf16[512,512]{1,0:T(8,128)(2,1)S(1)}, u32[]{:S(2)}, u32[]{:S(2)}) collective-permute-start(bf16[512,512]{1,0:T(8,128)(2,1)S(1)} %collective-permute-done.39.piece_ref), channel_id=1, source_target_pairs={{0,4},{8,0},{16,8},{24,16},{28,24},{20,28},{12,20},{4,12},{1,5},{9... | collective-permute-start | bytes 1572872 | tf_op jit(solution)/shard_map/ppermute | solution.py:192
  252.8 22.5 %collective-permute-start.44 = (bf16[512,512]{1,0:T(8,128)(2,1)S(1)}, bf16[512,512]{1,0:T(8,128)(2,1)S(1)}, u32[]{:S(2)}, u32[]{:S(2)}) collective-permute-start(bf16[512,512]{1,0:T(8,128)(2,1)S(1)} %collective-permute-done.40.piece_ref), channel_id=1, source_target_pairs={{0,8},{8,16},{16,24},{24,28},{28,20},{20,12},{12,4},{4,0},{1,9},{9... | collective-permute-start | bytes 1572872 | tf_op jit(solution)/shard_map/ppermute | solution.py:192
  258.9 22.5 %collective-permute-start.42 = (bf16[512,512]{1,0:T(8,128)(2,1)S(1)}, bf16[512,512]{1,0:T(8,128)(2,1)S(1)}, u32[]{:S(2)}, u32[]{:S(2)}) collective-permute-start(bf16[512,512]{1,0:T(8,128)(2,1)S(1)} %collective-permute-done.38.piece_ref), channel_id=1, source_target_pairs={{0,4},{8,0},{16,8},{24,16},{28,24},{20,28},{12,20},{4,12},{1,5},{9... | collective-permute-start | bytes 1572872 | tf_op jit(solution)/shard_map/ppermute | solution.py:192
  264.0 22.5 %collective-permute-start.49 = (bf16[512,512]{1,0:T(8,128)(2,1)S(1)}, bf16[512,512]{1,0:T(8,128)(2,1)S(1)}, u32[]{:S(2)}, u32[]{:S(2)}) collective-permute-start(bf16[512,512]{1,0:T(8,128)(2,1)S(1)} %collective-permute-done.45.piece_ref), channel_id=1, source_target_pairs={{0,8},{8,16},{16,24},{24,28},{28,20},{20,12},{12,4},{4,0},{1,9},{9... | collective-permute-start | bytes 1572872 | tf_op jit(solution)/shard_map/ppermute | solution.py:192
  270.2 22.5 %collective-permute-start.47 = (bf16[512,512]{1,0:T(8,128)(2,1)S(1)}, bf16[512,512]{1,0:T(8,128)(2,1)S(1)}, u32[]{:S(2)}, u32[]{:S(2)}) collective-permute-start(bf16[512,512]{1,0:T(8,128)(2,1)S(1)} %collective-permute-done.43.piece_ref), channel_id=1, source_target_pairs={{0,4},{8,0},{16,8},{24,16},{28,24},{20,28},{12,20},{4,12},{1,5},{9... | collective-permute-start | bytes 1572872 | tf_op jit(solution)/shard_map/ppermute | solution.py:192
  275.3 22.5 %collective-permute-start.48 = (bf16[512,512]{1,0:T(8,128)(2,1)S(1)}, bf16[512,512]{1,0:T(8,128)(2,1)S(1)}, u32[]{:S(2)}, u32[]{:S(2)}) collective-permute-start(bf16[512,512]{1,0:T(8,128)(2,1)S(1)} %collective-permute-done.44.piece_ref), channel_id=1, source_target_pairs={{0,8},{8,16},{16,24},{24,28},{28,20},{20,12},{12,4},{4,0},{1,9},{9... | collective-permute-start | bytes 1572872 | tf_op jit(solution)/shard_map/ppermute | solution.py:192
  281.4 22.5 %collective-permute-start.46 = (bf16[512,512]{1,0:T(8,128)(2,1)S(1)}, bf16[512,512]{1,0:T(8,128)(2,1)S(1)}, u32[]{:S(2)}, u32[]{:S(2)}) collective-permute-start(bf16[512,512]{1,0:T(8,128)(2,1)S(1)} %collective-permute-done.42.piece_ref), channel_id=1, source_target_pairs={{0,4},{8,0},{16,8},{24,16},{28,24},{20,28},{12,20},{4,12},{1,5},{9... | collective-permute-start | bytes 1572872 | tf_op jit(solution)/shard_map/ppermute | solution.py:192
  (40 other events, 761.3 us)

commit v4 on v3

--- a/solution.py
+++ b/solution.py
@@ -32,8 +32,10 @@
         jnp.float32
     )
     own = jnp.sum(onehot, axis=0)
-    before = lax.ppermute(own, "dp", [(d, d + 1) for d in range(count - 1)])
-    after = lax.ppermute(own, "dp", [(d + 1, d) for d in range(count - 1)])
+    before = lax.ppermute(own, "dp", [(d, d ^ 1) for d in range(count)])
+    after = lax.ppermute(
+        own, "dp", [(d, d - 1 + 2 * (d % 2)) for d in range(1, count - 1)]
+    )
     lengths = jnp.maximum(own + before + after, 1.0)
     grouped = rewards.reshape(count_all // GROUP, GROUP)
     center = jnp.mean(grouped, axis=1, keepdims=True)
@@ -92,16 +94,29 @@
     return walk
 
 
+def place_of(d, count):
+    inner = count // OUTER
+    o, i = lax.div(d, inner), lax.rem(d, inner)
+    turn = OUTER - 1 - o
+    along = jnp.where(lax.rem(turn, 2) == 0, i - 1, inner - 1 - i)
+    return jnp.where(i == 0, o, OUTER + turn * (inner - 1) + along)
+
+
+def at_place(p, count):
+    inner = count // OUTER
+    q = jnp.maximum(p - OUTER, 0)
+    turn, along = lax.div(q, inner - 1), lax.rem(q, inner - 1)
+    i = jnp.where(lax.rem(turn, 2) == 0, 1 + along, inner - 1 - along)
+    return jnp.where(p < OUTER, p * inner, (OUTER - 1 - turn) * inner + i)
+
+
 def shards(attn_out, out_grad, completion_ids, rewards, master, moment_one, moment_two):
     count = lax.psum(1, "dp")
     rows, wide = master.shape
     walk = cycle(count)
-    places = [walk.index(d) for d in range(count)]
     me = lax.axis_index("dp")
-    table = jnp.asarray(
-        [[walk[(places[d] + k) % count] for k in range(count)] for d in range(count)], jnp.int32
-    )[me]
-    owners = [table[k] for k in range(count)]
+    here = place_of(me, count)
+    owners = [at_place(lax.rem(here + k, count), count) for k in range(count)]
     pairs = {
         turn: [(walk[p], walk[(p + turn) % count]) for p in range(count)] for turn in (1, -1)
     }

time: 344 us -> 336 us (0.977)
  between operations: 6.65 us -> 1.83 us
  transfers between devices with their start and end apart: 58 -> 58, of which waited for: 50 -> 50; matrix products, arithmetic and copies ran while one was open for 10% -> 9% of each run, Pallas kernels for 10% -> 10%
where the time goes in v4:
time: 336 us
  waiting for transfers between devices  177 us (53%)
  starting transfers between devices  84.6 us (25%)
  Pallas kernels  33.5 us (10%)
  matrix products  24.4 us (7%)
  other arithmetic  12.9 us (4%)
    ppermute x28, waiting for transfers between devices, shards(): arrived = lax.ppermute(moving[c], 'dp', pairs[turns[c]])  97.4 us
    ppermute x28, waiting for transfers between devices, shards(): moving[c] = lax.ppermute(moving[c], 'dp', pairs[turn])  80 us
    ppermute x28, starting transfers between devices, shards(): moving[c] = lax.ppermute(moving[c], 'dp', pairs[turn])  42.9 us
    ppermute x28, starting transfers between devices, shards(): arrived = lax.ppermute(moving[c], 'dp', pairs[turns[c]])  38.1 us
    pallas_call x40, Pallas kernels, place(): pl.pallas_call(body, out_shape=jax.ShapeDtypeStruct(shape, whole.dtype),...  33.5 us
    dot_general x32, matrix products, contract_tokens(): lax.dot_general(left, right, (((0,), (0,)), ((), ())), preferred_element_...  23.4 us
  transfers between devices with their start and end apart: 58, of which 50 were waited for; matrix products, arithmetic and copies ran while one was open for 9% of the time, Pallas kernels for 10%

profile of v4, /device:TPU:0, one launch (start us, length us, event | category | flops | bytes accessed | tf_op | source)
XLA Modules:
  0.0 335.7 jit_solution(14748101899679361248)
XLA Ops:
  1.4 3.0 collective-permute-start
  12.9 5.3 %collective-permute-start.3 = (bf16[512,512]{1,0:T(8,128)(2,1)S(1)}, bf16[512,512]{1,0:T(8,128)(2,1)S(1)}, u32[]{:S(2)}, u32[]{:S(2)}) collective-permute-start(bf16[512,512]{1,0:T(8,128)(2,1)S(1)} %convolution_convert_fusion.28), channel_id=1, source_target_pairs={{0,8},{8,16},{16,24},{24,28},{28,20},{20,12},{12,4},{4,0},{1,9},{9... | collective-permute-start | bytes 1572872 | tf_op jit(solution)/shard_map/ppermute | solution.py:159
  21.4 9.2 %collective-permute-done.3 = bf16[512,512]{1,0:T(8,128)(2,1)S(1)} collective-permute-done((bf16[512,512]{1,0:T(8,128)(2,1)S(1)}, bf16[512,512]{1,0:T(8,128)(2,1)S(1)}, u32[]{:S(2)}, u32[]{:S(2)}) %collective-permute-start.3) | collective-permute-done | bytes 524320 | tf_op jit(solution)/shard_map/ppermute | solution.py:159
  59.4 6.5 %collective-permute-done.11 = bf16[512,512]{1,0:T(8,128)(2,1)S(1)} collective-permute-done((bf16[512,512]{1,0:T(8,128)(2,1)S(1)}, bf16[512,512]{1,0:T(8,128)(2,1)S(1)}, u32[]{:S(2)}, u32[]{:S(2)}) %collective-permute-start.11) | collective-permute-done | bytes 524320 | tf_op jit(solution)/shard_map/ppermute | solution.py:159
  69.8 7.4 %collective-permute-done.25 = bf16[512,512]{1,0:T(8,128)(2,1)S(1)} collective-permute-done((bf16[512,512]{1,0:T(8,128)(2,1)S(1)}, bf16[512,512]{1,0:T(8,128)(2,1)S(1)}, u32[]{:S(2)}, u32[]{:S(2)}) %collective-permute-start.25) | collective-permute-done | bytes 524320 | tf_op jit(solution)/shard_map/ppermute | solution.py:159
  81.0 7.4 %collective-permute-done.12 = bf16[512,512]{1,0:T(8,128)(2,1)S(1)} collective-permute-done((bf16[512,512]{1,0:T(8,128)(2,1)S(1)}, bf16[512,512]{1,0:T(8,128)(2,1)S(1)}, u32[]{:S(2)}, u32[]{:S(2)}) %collective-permute-start.12) | collective-permute-done | bytes 524320 | tf_op jit(solution)/shard_map/ppermute | solution.py:159
  92.3 7.4 %collective-permute-done.26 = bf16[512,512]{1,0:T(8,128)(2,1)S(1)} collective-permute-done((bf16[512,512]{1,0:T(8,128)(2,1)S(1)}, bf16[512,512]{1,0:T(8,128)(2,1)S(1)}, u32[]{:S(2)}, u32[]{:S(2)}) %collective-permute-start.26) | collective-permute-done | bytes 524320 | tf_op jit(solution)/shard_map/ppermute | solution.py:159
  103.5 7.4 %collective-permute-done.13 = bf16[512,512]{1,0:T(8,128)(2,1)S(1)} collective-permute-done((bf16[512,512]{1,0:T(8,128)(2,1)S(1)}, bf16[512,512]{1,0:T(8,128)(2,1)S(1)}, u32[]{:S(2)}, u32[]{:S(2)}) %collective-permute-start.13) | collective-permute-done | bytes 524320 | tf_op jit(solution)/shard_map/ppermute | solution.py:159
  114.8 7.4 %collective-permute-done.27 = bf16[512,512]{1,0:T(8,128)(2,1)S(1)} collective-permute-done((bf16[512,512]{1,0:T(8,128)(2,1)S(1)}, bf16[512,512]{1,0:T(8,128)(2,1)S(1)}, u32[]{:S(2)}, u32[]{:S(2)}) %collective-permute-start.27) | collective-permute-done | bytes 524320 | tf_op jit(solution)/shard_map/ppermute | solution.py:159
  126.0 7.4 %collective-permute-done.14 = bf16[512,512]{1,0:T(8,128)(2,1)S(1)} collective-permute-done((bf16[512,512]{1,0:T(8,128)(2,1)S(1)}, bf16[512,512]{1,0:T(8,128)(2,1)S(1)}, u32[]{:S(2)}, u32[]{:S(2)}) %collective-permute-start.14) | collective-permute-done | bytes 524320 | tf_op jit(solution)/shard_map/ppermute | solution.py:159
  137.2 7.4 %collective-permute-done.28 = bf16[512,512]{1,0:T(8,128)(2,1)S(1)} collective-permute-done((bf16[512,512]{1,0:T(8,128)(2,1)S(1)}, bf16[512,512]{1,0:T(8,128)(2,1)S(1)}, u32[]{:S(2)}, u32[]{:S(2)}) %collective-permute-start.28) | collective-permute-done | bytes 524320 | tf_op jit(solution)/shard_map/ppermute | solution.py:159
  148.5 7.4 %collective-permute-done.15 = bf16[512,512]{1,0:T(8,128)(2,1)S(1)} collective-permute-done((bf16[512,512]{1,0:T(8,128)(2,1)S(1)}, bf16[512,512]{1,0:T(8,128)(2,1)S(1)}, u32[]{:S(2)}, u32[]{:S(2)}) %collective-permute-start.15) | collective-permute-done | bytes 524320 | tf_op jit(solution)/shard_map/ppermute | solution.py:159
  159.7 7.4 %collective-permute-done.29 = bf16[512,512]{1,0:T(8,128)(2,1)S(1)} collective-permute-done((bf16[512,512]{1,0:T(8,128)(2,1)S(1)}, bf16[512,512]{1,0:T(8,128)(2,1)S(1)}, u32[]{:S(2)}, u32[]{:S(2)}) %collective-permute-start.29) | collective-permute-done | bytes 524320 | tf_op jit(solution)/shard_map/ppermute | solution.py:159
  173.3 5.0 %collective-permute-done.16 = bf16[512,512]{1,0:T(8,128)(2,1)S(1)} collective-permute-done((bf16[512,512]{1,0:T(8,128)(2,1)S(1)}, bf16[512,512]{1,0:T(8,128)(2,1)S(1)}, u32[]{:S(2)}, u32[]{:S(2)}) %collective-permute-start.16) | collective-permute-done | bytes 524320 | tf_op jit(solution)/shard_map/ppermute | solution.py:159
  186.4 3.1 collective-permute-done.33.piece_ref
  197.5 3.2 collective-permute-done.32.piece_ref
  220.0 3.2 collective-permute-done.36.piece_ref
  242.5 3.2 collective-permute-done.40.piece_ref
  265.0 3.2 collective-permute-done.44.piece_ref
  280.2 5.4 %collective-permute-done.47.piece_ref = bf16[512,512]{1,0:T(8,128)(2,1)S(1)} collective-permute-done((bf16[512,512]{1,0:T(8,128)(2,1)S(1)}, bf16[512,512]{1,0:T(8,128)(2,1)S(1)}, u32[]{:S(2)}, u32[]{:S(2)}) %collective-permute-start.47) | collective-permute-done | bytes 524320 | tf_op jit(solution)/shard_map/ppermute | solution.py:207
  298.7 3.2 collective-permute-done.53.piece_ref
  302.7 3.9 %collective-permute-done.51.piece_ref = bf16[512,512]{1,0:T(8,128)(2,1)S(1)} collective-permute-done((bf16[512,512]{1,0:T(8,128)(2,1)S(1)}, bf16[512,512]{1,0:T(8,128)(2,1)S(1)}, u32[]{:S(2)}, u32[]{:S(2)}) %collective-permute-start.51) | collective-permute-done | bytes 524320 | tf_op jit(solution)/shard_map/ppermute | solution.py:207
  310.3 3.6 %collective-permute-done.50.piece_ref = bf16[512,512]{1,0:T(8,128)(2,1)S(1)} collective-permute-done((bf16[512,512]{1,0:T(8,128)(2,1)S(1)}, bf16[512,512]{1,0:T(8,128)(2,1)S(1)}, u32[]{:S(2)}, u32[]{:S(2)}) %collective-permute-start.50) | collective-permute-done | bytes 524320 | tf_op jit(solution)/shard_map/ppermute | solution.py:207
  319.6 6.9 %collective-permute-done.57.piece_ref = bf16[512,512]{1,0:T(8,128)(2,1)S(1)} collective-permute-done((bf16[512,512]{1,0:T(8,128)(2,1)S(1)}, bf16[512,512]{1,0:T(8,128)(2,1)S(1)}, u32[]{:S(2)}, u32[]{:S(2)}) %collective-permute-start.57) | collective-permute-done | bytes 524320 | tf_op jit(solution)/shard_map/ppermute | solution.py:207
  (222 shorter events, 199.3 us)
Async XLA Ops:
  18.5 25.3 %collective-permute-start.17 = (bf16[512,512]{1,0:T(8,128)(2,1)S(1)}, bf16[512,512]{1,0:T(8,128)(2,1)S(1)}, u32[]{:S(2)}, u32[]{:S(2)}) collective-permute-start(bf16[512,512]{1,0:T(8,128)(2,1)S(1)} %convolution_convert_fusion.29), channel_id=1, source_target_pairs={{0,4},{8,0},{16,8},{24,16},{28,24},{20,28},{12,20},{4,12},{1,5},{9... | collective-permute-start | bytes 1572872 | tf_op jit(solution)/shard_map/ppermute | solution.py:159
  18.6 27.5 %collective-permute-start.10 = (bf16[512,512]{1,0:T(8,128)(2,1)S(1)}, bf16[512,512]{1,0:T(8,128)(2,1)S(1)}, u32[]{:S(2)}, u32[]{:S(2)}) collective-permute-start(bf16[512,512]{1,0:T(8,128)(2,1)S(1)} %convolution_convert_fusion.30), channel_id=1, source_target_pairs={{0,8},{8,16},{16,24},{24,28},{28,20},{20,12},{12,4},{4,0},{1,9},{9... | collective-permute-start | bytes 1572872 | tf_op jit(solution)/shard_map/ppermute | solution.py:159
  20.6 31.2 %collective-permute-start.2 = (bf16[512,512]{1,0:T(8,128)(2,1)S(1)}, bf16[512,512]{1,0:T(8,128)(2,1)S(1)}, u32[]{:S(2)}, u32[]{:S(2)}) collective-permute-start(bf16[512,512]{1,0:T(8,128)(2,1)S(1)} %convolution_convert_fusion.31), channel_id=1, source_target_pairs={{0,4},{8,0},{16,8},{24,16},{28,24},{20,28},{12,20},{4,12},{1,5},{9... | collective-permute-start | bytes 1572872 | tf_op jit(solution)/shard_map/ppermute | solution.py:159
  66.1 22.3 %collective-permute-start.12 = (bf16[512,512]{1,0:T(8,128)(2,1)S(1)}, bf16[512,512]{1,0:T(8,128)(2,1)S(1)}, u32[]{:S(2)}, u32[]{:S(2)}) collective-permute-start(bf16[512,512]{1,0:T(8,128)(2,1)S(1)} %add_convert_fusion.16), channel_id=1, source_target_pairs={{0,8},{8,16},{16,24},{24,28},{28,20},{20,12},{12,4},{4,0},{1,9},{9... | collective-permute-start | bytes 1572872 | tf_op jit(solution)/shard_map/ppermute | solution.py:159
  99.8 22.3 %collective-permute-start.27 = (bf16[512,512]{1,0:T(8,128)(2,1)S(1)}, bf16[512,512]{1,0:T(8,128)(2,1)S(1)}, u32[]{:S(2)}, u32[]{:S(2)}) collective-permute-start(bf16[512,512]{1,0:T(8,128)(2,1)S(1)} %add_convert_fusion.2), channel_id=1, source_target_pairs={{0,8},{8,16},{16,24},{24,28},{28,20},{20,12},{12,4},{4,0},{1,9},{9... | collective-permute-start | bytes 1572872 | tf_op jit(solution)/shard_map/ppermute | solution.py:159
  122.3 22.3 %collective-permute-start.28 = (bf16[512,512]{1,0:T(8,128)(2,1)S(1)}, bf16[512,512]{1,0:T(8,128)(2,1)S(1)}, u32[]{:S(2)}, u32[]{:S(2)}) collective-permute-start(bf16[512,512]{1,0:T(8,128)(2,1)S(1)} %add_convert_fusion.1), channel_id=1, source_target_pairs={{0,8},{8,16},{16,24},{24,28},{28,20},{20,12},{12,4},{4,0},{1,9},{9... | collective-permute-start | bytes 1572872 | tf_op jit(solution)/shard_map/ppermute | solution.py:159
  144.8 22.3 %collective-permute-start.29 = (bf16[512,512]{1,0:T(8,128)(2,1)S(1)}, bf16[512,512]{1,0:T(8,128)(2,1)S(1)}, u32[]{:S(2)}, u32[]{:S(2)}) collective-permute-start(bf16[512,512]{1,0:T(8,128)(2,1)S(1)} %add_convert_fusion), channel_id=1, source_target_pairs={{0,8},{8,16},{16,24},{24,28},{28,20},{20,12},{12,4},{4,0},{1,9},{9... | collective-permute-start | bytes 1572872 | tf_op jit(solution)/shard_map/ppermute | solution.py:159
  184.6 22.3 %collective-permute-start.30 = (bf16[512,512]{1,0:T(8,128)(2,1)S(1)}, bf16[512,512]{1,0:T(8,128)(2,1)S(1)}, u32[]{:S(2)}, u32[]{:S(2)}) collective-permute-start(bf16[512,512]{1,0:T(8,128)(2,1)S(1)} %get-tuple-element.195.piece_ref), channel_id=1, source_target_pairs={{0,4},{8,0},{16,8},{24,16},{28,24},{20,28},{12,20},{4,12},{1,5},{9... | collective-permute-start | bytes 1572872 | tf_op jit(solution)/shard_map/ppermute | solution.py:207
  189.5 22.5 %collective-permute-start.37 = (bf16[512,512]{1,0:T(8,128)(2,1)S(1)}, bf16[512,512]{1,0:T(8,128)(2,1)S(1)}, u32[]{:S(2)}, u32[]{:S(2)}) collective-permute-start(bf16[512,512]{1,0:T(8,128)(2,1)S(1)} %collective-permute-done.33.piece_ref), channel_id=1, source_target_pairs={{0,8},{8,16},{16,24},{24,28},{28,20},{20,12},{12,4},{4,0},{1,9},{9... | collective-permute-start | bytes 1572872 | tf_op jit(solution)/shard_map/ppermute | solution.py:207
  195.7 22.5 %collective-permute-start.35 = (bf16[512,512]{1,0:T(8,128)(2,1)S(1)}, bf16[512,512]{1,0:T(8,128)(2,1)S(1)}, u32[]{:S(2)}, u32[]{:S(2)}) collective-permute-start(bf16[512,512]{1,0:T(8,128)(2,1)S(1)} %collective-permute-done.31.piece_ref), channel_id=1, source_target_pairs={{0,4},{8,0},{16,8},{24,16},{28,24},{20,28},{12,20},{4,12},{1,5},{9... | collective-permute-start | bytes 1572872 | tf_op jit(solution)/shard_map/ppermute | solution.py:207
  200.8 22.5 %collective-permute-start.36 = (bf16[512,512]{1,0:T(8,128)(2,1)S(1)}, bf16[512,512]{1,0:T(8,128)(2,1)S(1)}, u32[]{:S(2)}, u32[]{:S(2)}) collective-permute-start(bf16[512,512]{1,0:T(8,128)(2,1)S(1)} %collective-permute-done.32.piece_ref), channel_id=1, source_target_pairs={{0,8},{8,16},{16,24},{24,28},{28,20},{20,12},{12,4},{4,0},{1,9},{9... | collective-permute-start | bytes 1572872 | tf_op jit(solution)/shard_map/ppermute | solution.py:207
  206.9 22.5 %collective-permute-start.34 = (bf16[512,512]{1,0:T(8,128)(2,1)S(1)}, bf16[512,512]{1,0:T(8,128)(2,1)S(1)}, u32[]{:S(2)}, u32[]{:S(2)}) collective-permute-start(bf16[512,512]{1,0:T(8,128)(2,1)S(1)} %collective-permute-done.30.piece_ref), channel_id=1, source_target_pairs={{0,4},{8,0},{16,8},{24,16},{28,24},{20,28},{12,20},{4,12},{1,5},{9... | collective-permute-start | bytes 1572872 | tf_op jit(solution)/shard_map/ppermute | solution.py:207
  212.0 22.5 %collective-permute-start.41 = (bf16[512,512]{1,0:T(8,128)(2,1)S(1)}, bf16[512,512]{1,0:T(8,128)(2,1)S(1)}, u32[]{:S(2)}, u32[]{:S(2)}) collective-permute-start(bf16[512,512]{1,0:T(8,128)(2,1)S(1)} %collective-permute-done.37.piece_ref), channel_id=1, source_target_pairs={{0,8},{8,16},{16,24},{24,28},{28,20},{20,12},{12,4},{4,0},{1,9},{9... | collective-permute-start | bytes 1572872 | tf_op jit(solution)/shard_map/ppermute | solution.py:207
  218.2 22.5 %collective-permute-start.39 = (bf16[512,512]{1,0:T(8,128)(2,1)S(1)}, bf16[512,512]{1,0:T(8,128)(2,1)S(1)}, u32[]{:S(2)}, u32[]{:S(2)}) collective-permute-start(bf16[512,512]{1,0:T(8,128)(2,1)S(1)} %collective-permute-done.35.piece_ref), channel_id=1, source_target_pairs={{0,4},{8,0},{16,8},{24,16},{28,24},{20,28},{12,20},{4,12},{1,5},{9... | collective-permute-start | bytes 1572872 | tf_op jit(solution)/shard_map/ppermute | solution.py:207
  223.2 22.5 %collective-permute-start.40 = (bf16[512,512]{1,0:T(8,128)(2,1)S(1)}, bf16[512,512]{1,0:T(8,128)(2,1)S(1)}, u32[]{:S(2)}, u32[]{:S(2)}) collective-permute-start(bf16[512,512]{1,0:T(8,128)(2,1)S(1)} %collective-permute-done.36.piece_ref), channel_id=1, source_target_pairs={{0,8},{8,16},{16,24},{24,28},{28,20},{20,12},{12,4},{4,0},{1,9},{9... | collective-permute-start | bytes 1572872 | tf_op jit(solution)/shard_map/ppermute | solution.py:207
  229.4 22.5 %collective-permute-start.38 = (bf16[512,512]{1,0:T(8,128)(2,1)S(1)}, bf16[512,512]{1,0:T(8,128)(2,1)S(1)}, u32[]{:S(2)}, u32[]{:S(2)}) collective-permute-start(bf16[512,512]{1,0:T(8,128)(2,1)S(1)} %collective-permute-done.34.piece_ref), channel_id=1, source_target_pairs={{0,4},{8,0},{16,8},{24,16},{28,24},{20,28},{12,20},{4,12},{1,5},{9... | collective-permute-start | bytes 1572872 | tf_op jit(solution)/shard_map/ppermute | solution.py:207
  234.5 22.5 %collective-permute-start.45 = (bf16[512,512]{1,0:T(8,128)(2,1)S(1)}, bf16[512,512]{1,0:T(8,128)(2,1)S(1)}, u32[]{:S(2)}, u32[]{:S(2)}) collective-permute-start(bf16[512,512]{1,0:T(8,128)(2,1)S(1)} %collective-permute-done.41.piece_ref), channel_id=1, source_target_pairs={{0,8},{8,16},{16,24},{24,28},{28,20},{20,12},{12,4},{4,0},{1,9},{9... | collective-permute-start | bytes 1572872 | tf_op jit(solution)/shard_map/ppermute | solution.py:207
  240.7 22.5 %collective-permute-start.43 = (bf16[512,512]{1,0:T(8,128)(2,1)S(1)}, bf16[512,512]{1,0:T(8,128)(2,1)S(1)}, u32[]{:S(2)}, u32[]{:S(2)}) collective-permute-start(bf16[512,512]{1,0:T(8,128)(2,1)S(1)} %collective-permute-done.39.piece_ref), channel_id=1, source_target_pairs={{0,4},{8,0},{16,8},{24,16},{28,24},{20,28},{12,20},{4,12},{1,5},{9... | collective-permute-start | bytes 1572872 | tf_op jit(solution)/shard_map/ppermute | solution.py:207
  245.7 22.5 %collective-permute-start.44 = (bf16[512,512]{1,0:T(8,128)(2,1)S(1)}, bf16[512,512]{1,0:T(8,128)(2,1)S(1)}, u32[]{:S(2)}, u32[]{:S(2)}) collective-permute-start(bf16[512,512]{1,0:T(8,128)(2,1)S(1)} %collective-permute-done.40.piece_ref), channel_id=1, source_target_pairs={{0,8},{8,16},{16,24},{24,28},{28,20},{20,12},{12,4},{4,0},{1,9},{9... | collective-permute-start | bytes 1572872 | tf_op jit(solution)/shard_map/ppermute | solution.py:207
  251.9 22.5 %collective-permute-start.42 = (bf16[512,512]{1,0:T(8,128)(2,1)S(1)}, bf16[512,512]{1,0:T(8,128)(2,1)S(1)}, u32[]{:S(2)}, u32[]{:S(2)}) collective-permute-start(bf16[512,512]{1,0:T(8,128)(2,1)S(1)} %collective-permute-done.38.piece_ref), channel_id=1, source_target_pairs={{0,4},{8,0},{16,8},{24,16},{28,24},{20,28},{12,20},{4,12},{1,5},{9... | collective-permute-start | bytes 1572872 | tf_op jit(solution)/shard_map/ppermute | solution.py:207
  257.0 22.5 %collective-permute-start.49 = (bf16[512,512]{1,0:T(8,128)(2,1)S(1)}, bf16[512,512]{1,0:T(8,128)(2,1)S(1)}, u32[]{:S(2)}, u32[]{:S(2)}) collective-permute-start(bf16[512,512]{1,0:T(8,128)(2,1)S(1)} %collective-permute-done.45.piece_ref), channel_id=1, source_target_pairs={{0,8},{8,16},{16,24},{24,28},{28,20},{20,12},{12,4},{4,0},{1,9},{9... | collective-permute-start | bytes 1572872 | tf_op jit(solution)/shard_map/ppermute | solution.py:207
  263.1 22.5 %collective-permute-start.47 = (bf16[512,512]{1,0:T(8,128)(2,1)S(1)}, bf16[512,512]{1,0:T(8,128)(2,1)S(1)}, u32[]{:S(2)}, u32[]{:S(2)}) collective-permute-start(bf16[512,512]{1,0:T(8,128)(2,1)S(1)} %collective-permute-done.43.piece_ref), channel_id=1, source_target_pairs={{0,4},{8,0},{16,8},{24,16},{28,24},{20,28},{12,20},{4,12},{1,5},{9... | collective-permute-start | bytes 1572872 | tf_op jit(solution)/shard_map/ppermute | solution.py:207
  268.2 22.5 %collective-permute-start.48 = (bf16[512,512]{1,0:T(8,128)(2,1)S(1)}, bf16[512,512]{1,0:T(8,128)(2,1)S(1)}, u32[]{:S(2)}, u32[]{:S(2)}) collective-permute-start(bf16[512,512]{1,0:T(8,128)(2,1)S(1)} %collective-permute-done.44.piece_ref), channel_id=1, source_target_pairs={{0,8},{8,16},{16,24},{24,28},{28,20},{20,12},{12,4},{4,0},{1,9},{9... | collective-permute-start | bytes 1572872 | tf_op jit(solution)/shard_map/ppermute | solution.py:207
  274.4 22.5 %collective-permute-start.46 = (bf16[512,512]{1,0:T(8,128)(2,1)S(1)}, bf16[512,512]{1,0:T(8,128)(2,1)S(1)}, u32[]{:S(2)}, u32[]{:S(2)}) collective-permute-start(bf16[512,512]{1,0:T(8,128)(2,1)S(1)} %collective-permute-done.42.piece_ref), channel_id=1, source_target_pairs={{0,4},{8,0},{16,8},{24,16},{28,24},{20,28},{12,20},{4,12},{1,5},{9... | collective-permute-start | bytes 1572872 | tf_op jit(solution)/shard_map/ppermute | solution.py:207
  (40 other events, 747.6 us)

commit v5 on v4

--- a/solution.py
+++ b/solution.py
@@ -12,10 +12,9 @@
 OUTER = 4
 CHUNKS = 4
 LAG = 2
-HOIST = 28
+FIRST = 16
 SPREAD = (1, 2, 3, 4)
-FREE = 1
-AHEAD = 3
+FREE = 2
 
 
 beta_one = 0.9
@@ -123,7 +122,9 @@
     token_weight = token_weights(completion_ids, rewards, count)
     part = wide // CHUNKS
     turns = [1 if index % 2 == 0 else -1 for index in range(CHUNKS)]
-    cols = [slice(index * part, (index + 1) * part) for index in range(CHUNKS)]
+    half = wide // 2
+    starts = [half * (index % 2) + part * (index // 2) for index in range(CHUNKS)]
+    cols = [slice(start, start + part) for start in starts]
     blocks = {}
 
     def weighted(k, gate):
@@ -155,22 +156,24 @@
             terms[number] = term(c, step + 1)
         return gate
 
+    gate = prepare(0, gate)
+    ready = 1
     for number, (step, c) in enumerate(events):
         arrived = lax.ppermute(moving[c], "dp", pairs[turns[c]])
-        if number == 0:
-            gate = prepare(0, gate)
         if number < FREE:
             arrived, gate = lax.optimization_barrier((arrived, gate))
         if number == 0:
-            for early in range(1, HOIST):
-                gate = prepare(early, gate)
+            while ready < min(FIRST, len(events)):
+                gate = prepare(ready, gate)
+                ready += 1
         moving[c] = arrived.astype(jnp.float32) + terms.pop(number).astype(jnp.float32)
         if step < count - 1:
             moving[c] = straight(moving[c].astype(jnp.bfloat16))
         if number < FREE:
             moving[c], gate = lax.optimization_barrier((moving[c], gate))
-        while len(terms) + number + 1 < min(max(HOIST, number + 1 + AHEAD), len(events)):
-            gate = prepare(len(terms) + number + 1, gate)
+        while number == FREE - 1 and ready < len(events):
+            gate = prepare(ready, gate)
+            ready += 1
     new_weights = jax.ShapeDtypeStruct((count * rows, wide), jnp.bfloat16)
     new_one = new_two = jax.ShapeDtypeStruct((rows, wide), jnp.float32)
     top = jnp.zeros((), jnp.int32)
@@ -194,7 +197,7 @@
     def put(into):
         c, step, piece = waiting.popleft()
         at = owners[-turns[c] * step % count]
-        return place(into, piece, at * rows, c * part)
+        return place(into, piece, at * rows, starts[c])
 
     for step in range(count):
         for c, turn in enumerate(turns):
@@ -207,8 +210,8 @@
                 moving[c] = lax.ppermute(moving[c], "dp", pairs[turn])
         for c in range(CHUNKS):
             if SPREAD[c] == step:
-                new_one = place(new_one, ones[c], top, c * part)
-                new_two = place(new_two, twos[c], top, c * part)
+                new_one = place(new_one, ones[c], top, starts[c])
+                new_two = place(new_two, twos[c], top, starts[c])
                 new_weights, new_one, new_two = lax.optimization_barrier(
                     (new_weights, new_one, new_two)
                 )

time: 336 us -> 335 us (level)
  transfers between devices with their start and end apart: 58 -> 58, of which waited for: 50 -> 42; matrix products, arithmetic and copies ran while one was open for 9% -> 9% of each run, Pallas kernels for 10% -> 10%
where the time goes in v5:
time: 335 us
  waiting for transfers between devices  176 us (53%)
  starting transfers between devices  85.2 us (25%)
  Pallas kernels  33.5 us (10%)
  matrix products  24.4 us (7%)
  other arithmetic  12.6 us (4%)
    ppermute x28, waiting for transfers between devices, shards(): arrived = lax.ppermute(moving[c], 'dp', pairs[turns[c]])  98.4 us
    ppermute x28, waiting for transfers between devices, shards(): moving[c] = lax.ppermute(moving[c], 'dp', pairs[turn])  77.8 us
    ppermute x28, starting transfers between devices, shards(): moving[c] = lax.ppermute(moving[c], 'dp', pairs[turn])  43.3 us
    ppermute x28, starting transfers between devices, shards(): arrived = lax.ppermute(moving[c], 'dp', pairs[turns[c]])  38.3 us
    pallas_call x40, Pallas kernels, place(): pl.pallas_call(body, out_shape=jax.ShapeDtypeStruct(shape, whole.dtype),...  33.5 us
    dot_general x32, matrix products, contract_tokens(): lax.dot_general(left, right, (((0,), (0,)), ((), ())), preferred_element_...  23.4 us
  transfers between devices with their start and end apart: 58, of which 42 were waited for; matrix products, arithmetic and copies ran while one was open for 9% of the time, Pallas kernels for 10%

profile of v5, /device:TPU:0, one launch (start us, length us, event | category | flops | bytes accessed | tf_op | source)
XLA Modules:
  0.0 334.9 jit_solution(16535439160282929456)
XLA Ops:
  1.4 3.0 collective-permute-start
  12.9 5.3 %collective-permute-start.3 = (bf16[512,512]{1,0:T(8,128)(2,1)S(1)}, bf16[512,512]{1,0:T(8,128)(2,1)S(1)}, u32[]{:S(2)}, u32[]{:S(2)}) collective-permute-start(bf16[512,512]{1,0:T(8,128)(2,1)S(1)} %convolution_convert_fusion.28), channel_id=1, source_target_pairs={{0,8},{8,16},{16,24},{24,28},{28,20},{20,12},{12,4},{4,0},{1,9},{9... | collective-permute-start | bytes 1572872 | tf_op jit(solution)/shard_map/ppermute | solution.py:162
  21.4 9.2 %collective-permute-done.3 = bf16[512,512]{1,0:T(8,128)(2,1)S(1)} collective-permute-done((bf16[512,512]{1,0:T(8,128)(2,1)S(1)}, bf16[512,512]{1,0:T(8,128)(2,1)S(1)}, u32[]{:S(2)}, u32[]{:S(2)}) %collective-permute-start.3) | collective-permute-done | bytes 524320 | tf_op jit(solution)/shard_map/ppermute | solution.py:162
  60.3 7.2 %collective-permute-done.12 = bf16[512,512]{1,0:T(8,128)(2,1)S(1)} collective-permute-done((bf16[512,512]{1,0:T(8,128)(2,1)S(1)}, bf16[512,512]{1,0:T(8,128)(2,1)S(1)}, u32[]{:S(2)}, u32[]{:S(2)}) %collective-permute-start.12) | collective-permute-done | bytes 524320 | tf_op jit(solution)/shard_map/ppermute | solution.py:162
  70.4 8.3 %collective-permute-done.25 = bf16[512,512]{1,0:T(8,128)(2,1)S(1)} collective-permute-done((bf16[512,512]{1,0:T(8,128)(2,1)S(1)}, bf16[512,512]{1,0:T(8,128)(2,1)S(1)}, u32[]{:S(2)}, u32[]{:S(2)}) %collective-permute-start.25) | collective-permute-done | bytes 524320 | tf_op jit(solution)/shard_map/ppermute | solution.py:162
  81.6 8.3 %collective-permute-done.13 = bf16[512,512]{1,0:T(8,128)(2,1)S(1)} collective-permute-done((bf16[512,512]{1,0:T(8,128)(2,1)S(1)}, bf16[512,512]{1,0:T(8,128)(2,1)S(1)}, u32[]{:S(2)}, u32[]{:S(2)}) %collective-permute-start.13) | collective-permute-done | bytes 524320 | tf_op jit(solution)/shard_map/ppermute | solution.py:162
  92.9 8.3 %collective-permute-done.26 = bf16[512,512]{1,0:T(8,128)(2,1)S(1)} collective-permute-done((bf16[512,512]{1,0:T(8,128)(2,1)S(1)}, bf16[512,512]{1,0:T(8,128)(2,1)S(1)}, u32[]{:S(2)}, u32[]{:S(2)}) %collective-permute-start.26) | collective-permute-done | bytes 524320 | tf_op jit(solution)/shard_map/ppermute | solution.py:162
  104.1 8.3 %collective-permute-done.14 = bf16[512,512]{1,0:T(8,128)(2,1)S(1)} collective-permute-done((bf16[512,512]{1,0:T(8,128)(2,1)S(1)}, bf16[512,512]{1,0:T(8,128)(2,1)S(1)}, u32[]{:S(2)}, u32[]{:S(2)}) %collective-permute-start.14) | collective-permute-done | bytes 524320 | tf_op jit(solution)/shard_map/ppermute | solution.py:162
  115.3 8.3 %collective-permute-done.27 = bf16[512,512]{1,0:T(8,128)(2,1)S(1)} collective-permute-done((bf16[512,512]{1,0:T(8,128)(2,1)S(1)}, bf16[512,512]{1,0:T(8,128)(2,1)S(1)}, u32[]{:S(2)}, u32[]{:S(2)}) %collective-permute-start.27) | collective-permute-done | bytes 524320 | tf_op jit(solution)/shard_map/ppermute | solution.py:162
  126.6 8.3 %collective-permute-done.15 = bf16[512,512]{1,0:T(8,128)(2,1)S(1)} collective-permute-done((bf16[512,512]{1,0:T(8,128)(2,1)S(1)}, bf16[512,512]{1,0:T(8,128)(2,1)S(1)}, u32[]{:S(2)}, u32[]{:S(2)}) %collective-permute-start.15) | collective-permute-done | bytes 524320 | tf_op jit(solution)/shard_map/ppermute | solution.py:162
  137.8 8.3 %collective-permute-done.28 = bf16[512,512]{1,0:T(8,128)(2,1)S(1)} collective-permute-done((bf16[512,512]{1,0:T(8,128)(2,1)S(1)}, bf16[512,512]{1,0:T(8,128)(2,1)S(1)}, u32[]{:S(2)}, u32[]{:S(2)}) %collective-permute-start.28) | collective-permute-done | bytes 524320 | tf_op jit(solution)/shard_map/ppermute | solution.py:162
  149.3 8.0 %collective-permute-done.16 = bf16[512,512]{1,0:T(8,128)(2,1)S(1)} collective-permute-done((bf16[512,512]{1,0:T(8,128)(2,1)S(1)}, bf16[512,512]{1,0:T(8,128)(2,1)S(1)}, u32[]{:S(2)}, u32[]{:S(2)}) %collective-permute-start.16) | collective-permute-done | bytes 524320 | tf_op jit(solution)/shard_map/ppermute | solution.py:162
  160.3 8.3 %collective-permute-done.29 = bf16[512,512]{1,0:T(8,128)(2,1)S(1)} collective-permute-done((bf16[512,512]{1,0:T(8,128)(2,1)S(1)}, bf16[512,512]{1,0:T(8,128)(2,1)S(1)}, u32[]{:S(2)}, u32[]{:S(2)}) %collective-permute-start.29) | collective-permute-done | bytes 524320 | tf_op jit(solution)/shard_map/ppermute | solution.py:162
  173.1 6.7 %collective-permute-done.17 = bf16[512,512]{1,0:T(8,128)(2,1)S(1)} collective-permute-done((bf16[512,512]{1,0:T(8,128)(2,1)S(1)}, bf16[512,512]{1,0:T(8,128)(2,1)S(1)}, u32[]{:S(2)}, u32[]{:S(2)}) %collective-permute-start.17) | collective-permute-done | bytes 524320 | tf_op jit(solution)/shard_map/ppermute | solution.py:162
  187.9 3.1 collective-permute-done.33.piece_ref
  199.0 3.3 collective-permute-done.32.piece_ref
  221.5 3.3 collective-permute-done.36.piece_ref
  244.0 3.3 collective-permute-done.40.piece_ref
  266.4 3.3 collective-permute-done.44.piece_ref
  281.7 5.4 %collective-permute-done.47.piece_ref = bf16[512,512]{1,0:T(8,128)(2,1)S(1)} collective-permute-done((bf16[512,512]{1,0:T(8,128)(2,1)S(1)}, bf16[512,512]{1,0:T(8,128)(2,1)S(1)}, u32[]{:S(2)}, u32[]{:S(2)}) %collective-permute-start.47) | collective-permute-done | bytes 524320 | tf_op jit(solution)/shard_map/ppermute | solution.py:210
  300.1 3.2 collective-permute-done.53.piece_ref
  306.6 4.4 %collective-permute-done.52.piece_ref = bf16[512,512]{1,0:T(8,128)(2,1)S(1)} collective-permute-done((bf16[512,512]{1,0:T(8,128)(2,1)S(1)}, bf16[512,512]{1,0:T(8,128)(2,1)S(1)}, u32[]{:S(2)}, u32[]{:S(2)}) %collective-permute-start.52) | collective-permute-done | bytes 524320 | tf_op jit(solution)/shard_map/ppermute | solution.py:210
  319.2 7.9 %collective-permute-done.57.piece_ref = bf16[512,512]{1,0:T(8,128)(2,1)S(1)} collective-permute-done((bf16[512,512]{1,0:T(8,128)(2,1)S(1)}, bf16[512,512]{1,0:T(8,128)(2,1)S(1)}, u32[]{:S(2)}, u32[]{:S(2)}) %collective-permute-start.57) | collective-permute-done | bytes 524320 | tf_op jit(solution)/shard_map/ppermute | solution.py:210
  329.1 3.6 %collective-permute-done.55.piece_ref = bf16[512,512]{1,0:T(8,128)(2,1)S(1)} collective-permute-done((bf16[512,512]{1,0:T(8,128)(2,1)S(1)}, bf16[512,512]{1,0:T(8,128)(2,1)S(1)}, u32[]{:S(2)}, u32[]{:S(2)}) %collective-permute-start.55) | collective-permute-done | bytes 524320 | tf_op jit(solution)/shard_map/ppermute | solution.py:210
  (222 shorter events, 186.8 us)
Async XLA Ops:
  18.6 26.7 %collective-permute-start.11 = (bf16[512,512]{1,0:T(8,128)(2,1)S(1)}, bf16[512,512]{1,0:T(8,128)(2,1)S(1)}, u32[]{:S(2)}, u32[]{:S(2)}) collective-permute-start(bf16[512,512]{1,0:T(8,128)(2,1)S(1)} %convolution_convert_fusion.30), channel_id=1, source_target_pairs={{0,8},{8,16},{16,24},{24,28},{28,20},{20,12},{12,4},{4,0},{1,9},{9... | collective-permute-start | bytes 1572872 | tf_op jit(solution)/shard_map/ppermute | solution.py:162
  20.6 30.5 %collective-permute-start.2 = (bf16[512,512]{1,0:T(8,128)(2,1)S(1)}, bf16[512,512]{1,0:T(8,128)(2,1)S(1)}, u32[]{:S(2)}, u32[]{:S(2)}) collective-permute-start(bf16[512,512]{1,0:T(8,128)(2,1)S(1)} %convolution_convert_fusion.31), channel_id=1, source_target_pairs={{0,4},{8,0},{16,8},{24,16},{28,24},{20,28},{12,20},{4,12},{1,5},{9... | collective-permute-start | bytes 1572872 | tf_op jit(solution)/shard_map/ppermute | solution.py:162
  67.6 22.3 %collective-permute-start.13 = (bf16[512,512]{1,0:T(8,128)(2,1)S(1)}, bf16[512,512]{1,0:T(8,128)(2,1)S(1)}, u32[]{:S(2)}, u32[]{:S(2)}) collective-permute-start(bf16[512,512]{1,0:T(8,128)(2,1)S(1)} %add_convert_fusion.14), channel_id=1, source_target_pairs={{0,8},{8,16},{16,24},{24,28},{28,20},{20,12},{12,4},{4,0},{1,9},{9... | collective-permute-start | bytes 1572872 | tf_op jit(solution)/shard_map/ppermute | solution.py:162
  78.9 22.3 %collective-permute-start.26 = (bf16[512,512]{1,0:T(8,128)(2,1)S(1)}, bf16[512,512]{1,0:T(8,128)(2,1)S(1)}, u32[]{:S(2)}, u32[]{:S(2)}) collective-permute-start(bf16[512,512]{1,0:T(8,128)(2,1)S(1)} %add_convert_fusion.3), channel_id=1, source_target_pairs={{0,8},{8,16},{16,24},{24,28},{28,20},{20,12},{12,4},{4,0},{1,9},{9... | collective-permute-start | bytes 1572872 | tf_op jit(solution)/shard_map/ppermute | solution.py:162
  123.8 22.3 %collective-permute-start.28 = (bf16[512,512]{1,0:T(8,128)(2,1)S(1)}, bf16[512,512]{1,0:T(8,128)(2,1)S(1)}, u32[]{:S(2)}, u32[]{:S(2)}) collective-permute-start(bf16[512,512]{1,0:T(8,128)(2,1)S(1)} %add_convert_fusion.1), channel_id=1, source_target_pairs={{0,8},{8,16},{16,24},{24,28},{28,20},{20,12},{12,4},{4,0},{1,9},{9... | collective-permute-start | bytes 1572872 | tf_op jit(solution)/shard_map/ppermute | solution.py:162
  126.5 22.6 %collective-permute-start.22 = (bf16[512,512]{1,0:T(8,128)(2,1)S(1)}, bf16[512,512]{1,0:T(8,128)(2,1)S(1)}, u32[]{:S(2)}, u32[]{:S(2)}) collective-permute-start(bf16[512,512]{1,0:T(8,128)(2,1)S(1)} %add_convert_fusion.6), channel_id=1, source_target_pairs={{0,4},{8,0},{16,8},{24,16},{28,24},{20,28},{12,20},{4,12},{1,5},{9... | collective-permute-start | bytes 1572872 | tf_op jit(solution)/shard_map/ppermute | solution.py:162
  137.8 22.3 %collective-permute-start.9 = (bf16[512,512]{1,0:T(8,128)(2,1)S(1)}, bf16[512,512]{1,0:T(8,128)(2,1)S(1)}, u32[]{:S(2)}, u32[]{:S(2)}) collective-permute-start(bf16[512,512]{1,0:T(8,128)(2,1)S(1)} %add_convert_fusion.17), channel_id=1, source_target_pairs={{0,4},{8,0},{16,8},{24,16},{28,24},{20,28},{12,20},{4,12},{1,5},{9... | collective-permute-start | bytes 1572872 | tf_op jit(solution)/shard_map/ppermute | solution.py:162
  186.1 22.3 %collective-permute-start.30 = (bf16[512,512]{1,0:T(8,128)(2,1)S(1)}, bf16[512,512]{1,0:T(8,128)(2,1)S(1)}, u32[]{:S(2)}, u32[]{:S(2)}) collective-permute-start(bf16[512,512]{1,0:T(8,128)(2,1)S(1)} %get-tuple-element.207.piece_ref), channel_id=1, source_target_pairs={{0,4},{8,0},{16,8},{24,16},{28,24},{20,28},{12,20},{4,12},{1,5},{9... | collective-permute-start | bytes 1572872 | tf_op jit(solution)/shard_map/ppermute | solution.py:210
  191.0 22.5 %collective-permute-start.37 = (bf16[512,512]{1,0:T(8,128)(2,1)S(1)}, bf16[512,512]{1,0:T(8,128)(2,1)S(1)}, u32[]{:S(2)}, u32[]{:S(2)}) collective-permute-start(bf16[512,512]{1,0:T(8,128)(2,1)S(1)} %collective-permute-done.33.piece_ref), channel_id=1, source_target_pairs={{0,8},{8,16},{16,24},{24,28},{28,20},{20,12},{12,4},{4,0},{1,9},{9... | collective-permute-start | bytes 1572872 | tf_op jit(solution)/shard_map/ppermute | solution.py:210
  197.2 22.5 %collective-permute-start.35 = (bf16[512,512]{1,0:T(8,128)(2,1)S(1)}, bf16[512,512]{1,0:T(8,128)(2,1)S(1)}, u32[]{:S(2)}, u32[]{:S(2)}) collective-permute-start(bf16[512,512]{1,0:T(8,128)(2,1)S(1)} %collective-permute-done.31.piece_ref), channel_id=1, source_target_pairs={{0,4},{8,0},{16,8},{24,16},{28,24},{20,28},{12,20},{4,12},{1,5},{9... | collective-permute-start | bytes 1572872 | tf_op jit(solution)/shard_map/ppermute | solution.py:210
  202.3 22.5 %collective-permute-start.36 = (bf16[512,512]{1,0:T(8,128)(2,1)S(1)}, bf16[512,512]{1,0:T(8,128)(2,1)S(1)}, u32[]{:S(2)}, u32[]{:S(2)}) collective-permute-start(bf16[512,512]{1,0:T(8,128)(2,1)S(1)} %collective-permute-done.32.piece_ref), channel_id=1, source_target_pairs={{0,8},{8,16},{16,24},{24,28},{28,20},{20,12},{12,4},{4,0},{1,9},{9... | collective-permute-start | bytes 1572872 | tf_op jit(solution)/shard_map/ppermute | solution.py:210
  208.4 22.5 %collective-permute-start.34 = (bf16[512,512]{1,0:T(8,128)(2,1)S(1)}, bf16[512,512]{1,0:T(8,128)(2,1)S(1)}, u32[]{:S(2)}, u32[]{:S(2)}) collective-permute-start(bf16[512,512]{1,0:T(8,128)(2,1)S(1)} %collective-permute-done.30.piece_ref), channel_id=1, source_target_pairs={{0,4},{8,0},{16,8},{24,16},{28,24},{20,28},{12,20},{4,12},{1,5},{9... | collective-permute-start | bytes 1572872 | tf_op jit(solution)/shard_map/ppermute | solution.py:210
  213.5 22.5 %collective-permute-start.41 = (bf16[512,512]{1,0:T(8,128)(2,1)S(1)}, bf16[512,512]{1,0:T(8,128)(2,1)S(1)}, u32[]{:S(2)}, u32[]{:S(2)}) collective-permute-start(bf16[512,512]{1,0:T(8,128)(2,1)S(1)} %collective-permute-done.37.piece_ref), channel_id=1, source_target_pairs={{0,8},{8,16},{16,24},{24,28},{28,20},{20,12},{12,4},{4,0},{1,9},{9... | collective-permute-start | bytes 1572872 | tf_op jit(solution)/shard_map/ppermute | solution.py:210
  219.7 22.5 %collective-permute-start.39 = (bf16[512,512]{1,0:T(8,128)(2,1)S(1)}, bf16[512,512]{1,0:T(8,128)(2,1)S(1)}, u32[]{:S(2)}, u32[]{:S(2)}) collective-permute-start(bf16[512,512]{1,0:T(8,128)(2,1)S(1)} %collective-permute-done.35.piece_ref), channel_id=1, source_target_pairs={{0,4},{8,0},{16,8},{24,16},{28,24},{20,28},{12,20},{4,12},{1,5},{9... | collective-permute-start | bytes 1572872 | tf_op jit(solution)/shard_map/ppermute | solution.py:210
  224.7 22.5 %collective-permute-start.40 = (bf16[512,512]{1,0:T(8,128)(2,1)S(1)}, bf16[512,512]{1,0:T(8,128)(2,1)S(1)}, u32[]{:S(2)}, u32[]{:S(2)}) collective-permute-start(bf16[512,512]{1,0:T(8,128)(2,1)S(1)} %collective-permute-done.36.piece_ref), channel_id=1, source_target_pairs={{0,8},{8,16},{16,24},{24,28},{28,20},{20,12},{12,4},{4,0},{1,9},{9... | collective-permute-start | bytes 1572872 | tf_op jit(solution)/shard_map/ppermute | solution.py:210
  230.9 22.5 %collective-permute-start.38 = (bf16[512,512]{1,0:T(8,128)(2,1)S(1)}, bf16[512,512]{1,0:T(8,128)(2,1)S(1)}, u32[]{:S(2)}, u32[]{:S(2)}) collective-permute-start(bf16[512,512]{1,0:T(8,128)(2,1)S(1)} %collective-permute-done.34.piece_ref), channel_id=1, source_target_pairs={{0,4},{8,0},{16,8},{24,16},{28,24},{20,28},{12,20},{4,12},{1,5},{9... | collective-permute-start | bytes 1572872 | tf_op jit(solution)/shard_map/ppermute | solution.py:210
  236.0 22.5 %collective-permute-start.45 = (bf16[512,512]{1,0:T(8,128)(2,1)S(1)}, bf16[512,512]{1,0:T(8,128)(2,1)S(1)}, u32[]{:S(2)}, u32[]{:S(2)}) collective-permute-start(bf16[512,512]{1,0:T(8,128)(2,1)S(1)} %collective-permute-done.41.piece_ref), channel_id=1, source_target_pairs={{0,8},{8,16},{16,24},{24,28},{28,20},{20,12},{12,4},{4,0},{1,9},{9... | collective-permute-start | bytes 1572872 | tf_op jit(solution)/shard_map/ppermute | solution.py:210
  242.2 22.5 %collective-permute-start.43 = (bf16[512,512]{1,0:T(8,128)(2,1)S(1)}, bf16[512,512]{1,0:T(8,128)(2,1)S(1)}, u32[]{:S(2)}, u32[]{:S(2)}) collective-permute-start(bf16[512,512]{1,0:T(8,128)(2,1)S(1)} %collective-permute-done.39.piece_ref), channel_id=1, source_target_pairs={{0,4},{8,0},{16,8},{24,16},{28,24},{20,28},{12,20},{4,12},{1,5},{9... | collective-permute-start | bytes 1572872 | tf_op jit(solution)/shard_map/ppermute | solution.py:210
  247.2 22.5 %collective-permute-start.44 = (bf16[512,512]{1,0:T(8,128)(2,1)S(1)}, bf16[512,512]{1,0:T(8,128)(2,1)S(1)}, u32[]{:S(2)}, u32[]{:S(2)}) collective-permute-start(bf16[512,512]{1,0:T(8,128)(2,1)S(1)} %collective-permute-done.40.piece_ref), channel_id=1, source_target_pairs={{0,8},{8,16},{16,24},{24,28},{28,20},{20,12},{12,4},{4,0},{1,9},{9... | collective-permute-start | bytes 1572872 | tf_op jit(solution)/shard_map/ppermute | solution.py:210
  253.4 22.5 %collective-permute-start.42 = (bf16[512,512]{1,0:T(8,128)(2,1)S(1)}, bf16[512,512]{1,0:T(8,128)(2,1)S(1)}, u32[]{:S(2)}, u32[]{:S(2)}) collective-permute-start(bf16[512,512]{1,0:T(8,128)(2,1)S(1)} %collective-permute-done.38.piece_ref), channel_id=1, source_target_pairs={{0,4},{8,0},{16,8},{24,16},{28,24},{20,28},{12,20},{4,12},{1,5},{9... | collective-permute-start | bytes 1572872 | tf_op jit(solution)/shard_map/ppermute | solution.py:210
  258.5 22.5 %collective-permute-start.49 = (bf16[512,512]{1,0:T(8,128)(2,1)S(1)}, bf16[512,512]{1,0:T(8,128)(2,1)S(1)}, u32[]{:S(2)}, u32[]{:S(2)}) collective-permute-start(bf16[512,512]{1,0:T(8,128)(2,1)S(1)} %collective-permute-done.45.piece_ref), channel_id=1, source_target_pairs={{0,8},{8,16},{16,24},{24,28},{28,20},{20,12},{12,4},{4,0},{1,9},{9... | collective-permute-start | bytes 1572872 | tf_op jit(solution)/shard_map/ppermute | solution.py:210
  264.6 22.5 %collective-permute-start.47 = (bf16[512,512]{1,0:T(8,128)(2,1)S(1)}, bf16[512,512]{1,0:T(8,128)(2,1)S(1)}, u32[]{:S(2)}, u32[]{:S(2)}) collective-permute-start(bf16[512,512]{1,0:T(8,128)(2,1)S(1)} %collective-permute-done.43.piece_ref), channel_id=1, source_target_pairs={{0,4},{8,0},{16,8},{24,16},{28,24},{20,28},{12,20},{4,12},{1,5},{9... | collective-permute-start | bytes 1572872 | tf_op jit(solution)/shard_map/ppermute | solution.py:210
  269.7 22.5 %collective-permute-start.48 = (bf16[512,512]{1,0:T(8,128)(2,1)S(1)}, bf16[512,512]{1,0:T(8,128)(2,1)S(1)}, u32[]{:S(2)}, u32[]{:S(2)}) collective-permute-start(bf16[512,512]{1,0:T(8,128)(2,1)S(1)} %collective-permute-done.44.piece_ref), channel_id=1, source_target_pairs={{0,8},{8,16},{16,24},{24,28},{28,20},{20,12},{12,4},{4,0},{1,9},{9... | collective-permute-start | bytes 1572872 | tf_op jit(solution)/shard_map/ppermute | solution.py:210
  275.9 22.5 %collective-permute-start.46 = (bf16[512,512]{1,0:T(8,128)(2,1)S(1)}, bf16[512,512]{1,0:T(8,128)(2,1)S(1)}, u32[]{:S(2)}, u32[]{:S(2)}) collective-permute-start(bf16[512,512]{1,0:T(8,128)(2,1)S(1)} %collective-permute-done.42.piece_ref), channel_id=1, source_target_pairs={{0,4},{8,0},{16,8},{24,16},{28,24},{20,28},{12,20},{4,12},{1,5},{9... | collective-permute-start | bytes 1572872 | tf_op jit(solution)/shard_map/ppermute | solution.py:210
  (40 other events, 745.8 us)

commit v6 on v5

--- a/solution.py
+++ b/solution.py
@@ -12,7 +12,8 @@
 OUTER = 4
 CHUNKS = 4
 LAG = 2
-FIRST = 16
+FIRST = 12
+SECOND = 20
 SPREAD = (1, 2, 3, 4)
 FREE = 2
 
@@ -80,7 +81,7 @@
         ),
         input_output_aliases={2: 0} if in_place else {},
         compiler_params=pltpu.CompilerParams(vmem_limit_bytes=1 << 20),
-        cost_estimate=pl.CostEstimate(flops=0, bytes_accessed=1024, transcendentals=0),
+        cost_estimate=pl.CostEstimate(flops=0, bytes_accessed=1 << 20, transcendentals=0),
     )(row.reshape(1), piece, *([whole] if in_place else []))
 
 
@@ -171,7 +172,7 @@
             moving[c] = straight(moving[c].astype(jnp.bfloat16))
         if number < FREE:
             moving[c], gate = lax.optimization_barrier((moving[c], gate))
-        while number == FREE - 1 and ready < len(events):
+        while number < FREE and ready < (len(events) if number == FREE - 1 else SECOND):
             gate = prepare(ready, gate)
             ready += 1
     new_weights = jax.ShapeDtypeStruct((count * rows, wide), jnp.bfloat16)

time: 335 us -> 335 us (level)
  no operation moved by 1% of the time
where the time goes in v6:
time: 335 us
  waiting for transfers between devices  176 us (53%)
  starting transfers between devices  85.2 us (25%)
  Pallas kernels  33.5 us (10%)
  matrix products  24.4 us (7%)
  other arithmetic  12.5 us (4%)
    ppermute x28, waiting for transfers between devices, shards(): arrived = lax.ppermute(moving[c], 'dp', pairs[turns[c]])  98.6 us
    ppermute x28, waiting for transfers between devices, shards(): moving[c] = lax.ppermute(moving[c], 'dp', pairs[turn])  77.7 us
    ppermute x28, starting transfers between devices, shards(): moving[c] = lax.ppermute(moving[c], 'dp', pairs[turn])  43.4 us
    ppermute x28, starting transfers between devices, shards(): arrived = lax.ppermute(moving[c], 'dp', pairs[turns[c]])  38.2 us
    pallas_call x40, Pallas kernels, place(): pl.pallas_call(body, out_shape=jax.ShapeDtypeStruct(shape, whole.dtype),...  33.5 us
    dot_general x32, matrix products, contract_tokens(): lax.dot_general(left, right, (((0,), (0,)), ((), ())), preferred_element_...  23.4 us
  transfers between devices with their start and end apart: 58, of which 42 were waited for; matrix products, arithmetic and copies ran while one was open for 9% of the time, Pallas kernels for 10%

profile of v6, /device:TPU:0, one launch (start us, length us, event | category | flops | bytes accessed | tf_op | source)
XLA Modules:
  0.0 334.9 jit_solution(5937682711976649182)
XLA Ops:
  1.4 3.0 collective-permute-start
  12.9 5.3 %collective-permute-start.3 = (bf16[512,512]{1,0:T(8,128)(2,1)S(1)}, bf16[512,512]{1,0:T(8,128)(2,1)S(1)}, u32[]{:S(2)}, u32[]{:S(2)}) collective-permute-start(bf16[512,512]{1,0:T(8,128)(2,1)S(1)} %convolution_convert_fusion.28), channel_id=1, source_target_pairs={{0,8},{8,16},{16,24},{24,28},{28,20},{20,12},{12,4},{4,0},{1,9},{9... | collective-permute-start | bytes 1572872 | tf_op jit(solution)/shard_map/ppermute | solution.py:163
  21.4 9.2 %collective-permute-done.3 = bf16[512,512]{1,0:T(8,128)(2,1)S(1)} collective-permute-done((bf16[512,512]{1,0:T(8,128)(2,1)S(1)}, bf16[512,512]{1,0:T(8,128)(2,1)S(1)}, u32[]{:S(2)}, u32[]{:S(2)}) %collective-permute-start.3) | collective-permute-done | bytes 524320 | tf_op jit(solution)/shard_map/ppermute | solution.py:163
  60.3 7.2 %collective-permute-done.12 = bf16[512,512]{1,0:T(8,128)(2,1)S(1)} collective-permute-done((bf16[512,512]{1,0:T(8,128)(2,1)S(1)}, bf16[512,512]{1,0:T(8,128)(2,1)S(1)}, u32[]{:S(2)}, u32[]{:S(2)}) %collective-permute-start.12) | collective-permute-done | bytes 524320 | tf_op jit(solution)/shard_map/ppermute | solution.py:163
  70.4 8.3 %collective-permute-done.25 = bf16[512,512]{1,0:T(8,128)(2,1)S(1)} collective-permute-done((bf16[512,512]{1,0:T(8,128)(2,1)S(1)}, bf16[512,512]{1,0:T(8,128)(2,1)S(1)}, u32[]{:S(2)}, u32[]{:S(2)}) %collective-permute-start.25) | collective-permute-done | bytes 524320 | tf_op jit(solution)/shard_map/ppermute | solution.py:163
  81.6 8.3 %collective-permute-done.13 = bf16[512,512]{1,0:T(8,128)(2,1)S(1)} collective-permute-done((bf16[512,512]{1,0:T(8,128)(2,1)S(1)}, bf16[512,512]{1,0:T(8,128)(2,1)S(1)}, u32[]{:S(2)}, u32[]{:S(2)}) %collective-permute-start.13) | collective-permute-done | bytes 524320 | tf_op jit(solution)/shard_map/ppermute | solution.py:163
  92.9 8.3 %collective-permute-done.26 = bf16[512,512]{1,0:T(8,128)(2,1)S(1)} collective-permute-done((bf16[512,512]{1,0:T(8,128)(2,1)S(1)}, bf16[512,512]{1,0:T(8,128)(2,1)S(1)}, u32[]{:S(2)}, u32[]{:S(2)}) %collective-permute-start.26) | collective-permute-done | bytes 524320 | tf_op jit(solution)/shard_map/ppermute | solution.py:163
  104.1 8.3 %collective-permute-done.14 = bf16[512,512]{1,0:T(8,128)(2,1)S(1)} collective-permute-done((bf16[512,512]{1,0:T(8,128)(2,1)S(1)}, bf16[512,512]{1,0:T(8,128)(2,1)S(1)}, u32[]{:S(2)}, u32[]{:S(2)}) %collective-permute-start.14) | collective-permute-done | bytes 524320 | tf_op jit(solution)/shard_map/ppermute | solution.py:163
  115.3 8.3 %collective-permute-done.27 = bf16[512,512]{1,0:T(8,128)(2,1)S(1)} collective-permute-done((bf16[512,512]{1,0:T(8,128)(2,1)S(1)}, bf16[512,512]{1,0:T(8,128)(2,1)S(1)}, u32[]{:S(2)}, u32[]{:S(2)}) %collective-permute-start.27) | collective-permute-done | bytes 524320 | tf_op jit(solution)/shard_map/ppermute | solution.py:163
  126.5 8.3 %collective-permute-done.15 = bf16[512,512]{1,0:T(8,128)(2,1)S(1)} collective-permute-done((bf16[512,512]{1,0:T(8,128)(2,1)S(1)}, bf16[512,512]{1,0:T(8,128)(2,1)S(1)}, u32[]{:S(2)}, u32[]{:S(2)}) %collective-permute-start.15) | collective-permute-done | bytes 524320 | tf_op jit(solution)/shard_map/ppermute | solution.py:163
  137.8 8.3 %collective-permute-done.28 = bf16[512,512]{1,0:T(8,128)(2,1)S(1)} collective-permute-done((bf16[512,512]{1,0:T(8,128)(2,1)S(1)}, bf16[512,512]{1,0:T(8,128)(2,1)S(1)}, u32[]{:S(2)}, u32[]{:S(2)}) %collective-permute-start.28) | collective-permute-done | bytes 524320 | tf_op jit(solution)/shard_map/ppermute | solution.py:163
  149.2 8.1 %collective-permute-done.16 = bf16[512,512]{1,0:T(8,128)(2,1)S(1)} collective-permute-done((bf16[512,512]{1,0:T(8,128)(2,1)S(1)}, bf16[512,512]{1,0:T(8,128)(2,1)S(1)}, u32[]{:S(2)}, u32[]{:S(2)}) %collective-permute-start.16) | collective-permute-done | bytes 524320 | tf_op jit(solution)/shard_map/ppermute | solution.py:163
  160.3 8.3 %collective-permute-done.29 = bf16[512,512]{1,0:T(8,128)(2,1)S(1)} collective-permute-done((bf16[512,512]{1,0:T(8,128)(2,1)S(1)}, bf16[512,512]{1,0:T(8,128)(2,1)S(1)}, u32[]{:S(2)}, u32[]{:S(2)}) %collective-permute-start.29) | collective-permute-done | bytes 524320 | tf_op jit(solution)/shard_map/ppermute | solution.py:163
  173.1 6.7 %collective-permute-done.17 = bf16[512,512]{1,0:T(8,128)(2,1)S(1)} collective-permute-done((bf16[512,512]{1,0:T(8,128)(2,1)S(1)}, bf16[512,512]{1,0:T(8,128)(2,1)S(1)}, u32[]{:S(2)}, u32[]{:S(2)}) %collective-permute-start.17) | collective-permute-done | bytes 524320 | tf_op jit(solution)/shard_map/ppermute | solution.py:163
  187.9 3.1 collective-permute-done.33.piece_ref
  199.0 3.2 collective-permute-done.32.piece_ref
  221.5 3.2 collective-permute-done.36.piece_ref
  243.9 3.2 collective-permute-done.40.piece_ref
  266.4 3.2 collective-permute-done.44.piece_ref
  281.7 5.4 %collective-permute-done.47.piece_ref = bf16[512,512]{1,0:T(8,128)(2,1)S(1)} collective-permute-done((bf16[512,512]{1,0:T(8,128)(2,1)S(1)}, bf16[512,512]{1,0:T(8,128)(2,1)S(1)}, u32[]{:S(2)}, u32[]{:S(2)}) %collective-permute-start.47) | collective-permute-done | bytes 524320 | tf_op jit(solution)/shard_map/ppermute | solution.py:211
  300.1 3.2 collective-permute-done.53.piece_ref
  306.6 4.3 %collective-permute-done.52.piece_ref = bf16[512,512]{1,0:T(8,128)(2,1)S(1)} collective-permute-done((bf16[512,512]{1,0:T(8,128)(2,1)S(1)}, bf16[512,512]{1,0:T(8,128)(2,1)S(1)}, u32[]{:S(2)}, u32[]{:S(2)}) %collective-permute-start.52) | collective-permute-done | bytes 524320 | tf_op jit(solution)/shard_map/ppermute | solution.py:211
  319.1 7.9 %collective-permute-done.57.piece_ref = bf16[512,512]{1,0:T(8,128)(2,1)S(1)} collective-permute-done((bf16[512,512]{1,0:T(8,128)(2,1)S(1)}, bf16[512,512]{1,0:T(8,128)(2,1)S(1)}, u32[]{:S(2)}, u32[]{:S(2)}) %collective-permute-start.57) | collective-permute-done | bytes 524320 | tf_op jit(solution)/shard_map/ppermute | solution.py:211
  329.1 3.6 %collective-permute-done.55.piece_ref = bf16[512,512]{1,0:T(8,128)(2,1)S(1)} collective-permute-done((bf16[512,512]{1,0:T(8,128)(2,1)S(1)}, bf16[512,512]{1,0:T(8,128)(2,1)S(1)}, u32[]{:S(2)}, u32[]{:S(2)}) %collective-permute-start.55) | collective-permute-done | bytes 524320 | tf_op jit(solution)/shard_map/ppermute | solution.py:211
  (222 shorter events, 186.8 us)
Async XLA Ops:
  18.6 26.7 %collective-permute-start.11 = (bf16[512,512]{1,0:T(8,128)(2,1)S(1)}, bf16[512,512]{1,0:T(8,128)(2,1)S(1)}, u32[]{:S(2)}, u32[]{:S(2)}) collective-permute-start(bf16[512,512]{1,0:T(8,128)(2,1)S(1)} %convolution_convert_fusion.30), channel_id=1, source_target_pairs={{0,8},{8,16},{16,24},{24,28},{28,20},{20,12},{12,4},{4,0},{1,9},{9... | collective-permute-start | bytes 1572872 | tf_op jit(solution)/shard_map/ppermute | solution.py:163
  20.6 30.4 %collective-permute-start.2 = (bf16[512,512]{1,0:T(8,128)(2,1)S(1)}, bf16[512,512]{1,0:T(8,128)(2,1)S(1)}, u32[]{:S(2)}, u32[]{:S(2)}) collective-permute-start(bf16[512,512]{1,0:T(8,128)(2,1)S(1)} %convolution_convert_fusion.31), channel_id=1, source_target_pairs={{0,4},{8,0},{16,8},{24,16},{28,24},{20,28},{12,20},{4,12},{1,5},{9... | collective-permute-start | bytes 1572872 | tf_op jit(solution)/shard_map/ppermute | solution.py:163
  67.6 22.3 %collective-permute-start.13 = (bf16[512,512]{1,0:T(8,128)(2,1)S(1)}, bf16[512,512]{1,0:T(8,128)(2,1)S(1)}, u32[]{:S(2)}, u32[]{:S(2)}) collective-permute-start(bf16[512,512]{1,0:T(8,128)(2,1)S(1)} %add_convert_fusion.14), channel_id=1, source_target_pairs={{0,8},{8,16},{16,24},{24,28},{28,20},{20,12},{12,4},{4,0},{1,9},{9... | collective-permute-start | bytes 1572872 | tf_op jit(solution)/shard_map/ppermute | solution.py:163
  70.3 22.3 %collective-permute-start.5 = (bf16[512,512]{1,0:T(8,128)(2,1)S(1)}, bf16[512,512]{1,0:T(8,128)(2,1)S(1)}, u32[]{:S(2)}, u32[]{:S(2)}) collective-permute-start(bf16[512,512]{1,0:T(8,128)(2,1)S(1)} %add_convert_fusion.22), channel_id=1, source_target_pairs={{0,4},{8,0},{16,8},{24,16},{28,24},{20,28},{12,20},{4,12},{1,5},{9... | collective-permute-start | bytes 1572872 | tf_op jit(solution)/shard_map/ppermute | solution.py:163
  78.8 22.3 %collective-permute-start.26 = (bf16[512,512]{1,0:T(8,128)(2,1)S(1)}, bf16[512,512]{1,0:T(8,128)(2,1)S(1)}, u32[]{:S(2)}, u32[]{:S(2)}) collective-permute-start(bf16[512,512]{1,0:T(8,128)(2,1)S(1)} %add_convert_fusion.3), channel_id=1, source_target_pairs={{0,8},{8,16},{16,24},{24,28},{28,20},{20,12},{12,4},{4,0},{1,9},{9... | collective-permute-start | bytes 1572872 | tf_op jit(solution)/shard_map/ppermute | solution.py:163
  126.5 22.5 %collective-permute-start.22 = (bf16[512,512]{1,0:T(8,128)(2,1)S(1)}, bf16[512,512]{1,0:T(8,128)(2,1)S(1)}, u32[]{:S(2)}, u32[]{:S(2)}) collective-permute-start(bf16[512,512]{1,0:T(8,128)(2,1)S(1)} %add_convert_fusion.6), channel_id=1, source_target_pairs={{0,4},{8,0},{16,8},{24,16},{28,24},{20,28},{12,20},{4,12},{1,5},{9... | collective-permute-start | bytes 1572872 | tf_op jit(solution)/shard_map/ppermute | solution.py:163
  137.7 22.3 %collective-permute-start.8 = (bf16[512,512]{1,0:T(8,128)(2,1)S(1)}, bf16[512,512]{1,0:T(8,128)(2,1)S(1)}, u32[]{:S(2)}, u32[]{:S(2)}) collective-permute-start(bf16[512,512]{1,0:T(8,128)(2,1)S(1)} %add_convert_fusion.18), channel_id=1, source_target_pairs={{0,4},{8,0},{16,8},{24,16},{28,24},{20,28},{12,20},{4,12},{1,5},{9... | collective-permute-start | bytes 1572872 | tf_op jit(solution)/shard_map/ppermute | solution.py:163
  186.1 22.3 %collective-permute-start.30 = (bf16[512,512]{1,0:T(8,128)(2,1)S(1)}, bf16[512,512]{1,0:T(8,128)(2,1)S(1)}, u32[]{:S(2)}, u32[]{:S(2)}) collective-permute-start(bf16[512,512]{1,0:T(8,128)(2,1)S(1)} %get-tuple-element.207.piece_ref), channel_id=1, source_target_pairs={{0,4},{8,0},{16,8},{24,16},{28,24},{20,28},{12,20},{4,12},{1,5},{9... | collective-permute-start | bytes 1572872 | tf_op jit(solution)/shard_map/ppermute | solution.py:211
  191.0 22.5 %collective-permute-start.37 = (bf16[512,512]{1,0:T(8,128)(2,1)S(1)}, bf16[512,512]{1,0:T(8,128)(2,1)S(1)}, u32[]{:S(2)}, u32[]{:S(2)}) collective-permute-start(bf16[512,512]{1,0:T(8,128)(2,1)S(1)} %collective-permute-done.33.piece_ref), channel_id=1, source_target_pairs={{0,8},{8,16},{16,24},{24,28},{28,20},{20,12},{12,4},{4,0},{1,9},{9... | collective-permute-start | bytes 1572872 | tf_op jit(solution)/shard_map/ppermute | solution.py:211
  197.2 22.5 %collective-permute-start.35 = (bf16[512,512]{1,0:T(8,128)(2,1)S(1)}, bf16[512,512]{1,0:T(8,128)(2,1)S(1)}, u32[]{:S(2)}, u32[]{:S(2)}) collective-permute-start(bf16[512,512]{1,0:T(8,128)(2,1)S(1)} %collective-permute-done.31.piece_ref), channel_id=1, source_target_pairs={{0,4},{8,0},{16,8},{24,16},{28,24},{20,28},{12,20},{4,12},{1,5},{9... | collective-permute-start | bytes 1572872 | tf_op jit(solution)/shard_map/ppermute | solution.py:211
  202.2 22.5 %collective-permute-start.36 = (bf16[512,512]{1,0:T(8,128)(2,1)S(1)}, bf16[512,512]{1,0:T(8,128)(2,1)S(1)}, u32[]{:S(2)}, u32[]{:S(2)}) collective-permute-start(bf16[512,512]{1,0:T(8,128)(2,1)S(1)} %collective-permute-done.32.piece_ref), channel_id=1, source_target_pairs={{0,8},{8,16},{16,24},{24,28},{28,20},{20,12},{12,4},{4,0},{1,9},{9... | collective-permute-start | bytes 1572872 | tf_op jit(solution)/shard_map/ppermute | solution.py:211
  208.4 22.5 %collective-permute-start.34 = (bf16[512,512]{1,0:T(8,128)(2,1)S(1)}, bf16[512,512]{1,0:T(8,128)(2,1)S(1)}, u32[]{:S(2)}, u32[]{:S(2)}) collective-permute-start(bf16[512,512]{1,0:T(8,128)(2,1)S(1)} %collective-permute-done.30.piece_ref), channel_id=1, source_target_pairs={{0,4},{8,0},{16,8},{24,16},{28,24},{20,28},{12,20},{4,12},{1,5},{9... | collective-permute-start | bytes 1572872 | tf_op jit(solution)/shard_map/ppermute | solution.py:211
  213.5 22.5 %collective-permute-start.41 = (bf16[512,512]{1,0:T(8,128)(2,1)S(1)}, bf16[512,512]{1,0:T(8,128)(2,1)S(1)}, u32[]{:S(2)}, u32[]{:S(2)}) collective-permute-start(bf16[512,512]{1,0:T(8,128)(2,1)S(1)} %collective-permute-done.37.piece_ref), channel_id=1, source_target_pairs={{0,8},{8,16},{16,24},{24,28},{28,20},{20,12},{12,4},{4,0},{1,9},{9... | collective-permute-start | bytes 1572872 | tf_op jit(solution)/shard_map/ppermute | solution.py:211
  219.6 22.5 %collective-permute-start.39 = (bf16[512,512]{1,0:T(8,128)(2,1)S(1)}, bf16[512,512]{1,0:T(8,128)(2,1)S(1)}, u32[]{:S(2)}, u32[]{:S(2)}) collective-permute-start(bf16[512,512]{1,0:T(8,128)(2,1)S(1)} %collective-permute-done.35.piece_ref), channel_id=1, source_target_pairs={{0,4},{8,0},{16,8},{24,16},{28,24},{20,28},{12,20},{4,12},{1,5},{9... | collective-permute-start | bytes 1572872 | tf_op jit(solution)/shard_map/ppermute | solution.py:211
  224.7 22.5 %collective-permute-start.40 = (bf16[512,512]{1,0:T(8,128)(2,1)S(1)}, bf16[512,512]{1,0:T(8,128)(2,1)S(1)}, u32[]{:S(2)}, u32[]{:S(2)}) collective-permute-start(bf16[512,512]{1,0:T(8,128)(2,1)S(1)} %collective-permute-done.36.piece_ref), channel_id=1, source_target_pairs={{0,8},{8,16},{16,24},{24,28},{28,20},{20,12},{12,4},{4,0},{1,9},{9... | collective-permute-start | bytes 1572872 | tf_op jit(solution)/shard_map/ppermute | solution.py:211
  230.9 22.5 %collective-permute-start.38 = (bf16[512,512]{1,0:T(8,128)(2,1)S(1)}, bf16[512,512]{1,0:T(8,128)(2,1)S(1)}, u32[]{:S(2)}, u32[]{:S(2)}) collective-permute-start(bf16[512,512]{1,0:T(8,128)(2,1)S(1)} %collective-permute-done.34.piece_ref), channel_id=1, source_target_pairs={{0,4},{8,0},{16,8},{24,16},{28,24},{20,28},{12,20},{4,12},{1,5},{9... | collective-permute-start | bytes 1572872 | tf_op jit(solution)/shard_map/ppermute | solution.py:211
  235.9 22.5 %collective-permute-start.45 = (bf16[512,512]{1,0:T(8,128)(2,1)S(1)}, bf16[512,512]{1,0:T(8,128)(2,1)S(1)}, u32[]{:S(2)}, u32[]{:S(2)}) collective-permute-start(bf16[512,512]{1,0:T(8,128)(2,1)S(1)} %collective-permute-done.41.piece_ref), channel_id=1, source_target_pairs={{0,8},{8,16},{16,24},{24,28},{28,20},{20,12},{12,4},{4,0},{1,9},{9... | collective-permute-start | bytes 1572872 | tf_op jit(solution)/shard_map/ppermute | solution.py:211
  242.1 22.5 %collective-permute-start.43 = (bf16[512,512]{1,0:T(8,128)(2,1)S(1)}, bf16[512,512]{1,0:T(8,128)(2,1)S(1)}, u32[]{:S(2)}, u32[]{:S(2)}) collective-permute-start(bf16[512,512]{1,0:T(8,128)(2,1)S(1)} %collective-permute-done.39.piece_ref), channel_id=1, source_target_pairs={{0,4},{8,0},{16,8},{24,16},{28,24},{20,28},{12,20},{4,12},{1,5},{9... | collective-permute-start | bytes 1572872 | tf_op jit(solution)/shard_map/ppermute | solution.py:211
  247.2 22.5 %collective-permute-start.44 = (bf16[512,512]{1,0:T(8,128)(2,1)S(1)}, bf16[512,512]{1,0:T(8,128)(2,1)S(1)}, u32[]{:S(2)}, u32[]{:S(2)}) collective-permute-start(bf16[512,512]{1,0:T(8,128)(2,1)S(1)} %collective-permute-done.40.piece_ref), channel_id=1, source_target_pairs={{0,8},{8,16},{16,24},{24,28},{28,20},{20,12},{12,4},{4,0},{1,9},{9... | collective-permute-start | bytes 1572872 | tf_op jit(solution)/shard_map/ppermute | solution.py:211
  253.3 22.5 %collective-permute-start.42 = (bf16[512,512]{1,0:T(8,128)(2,1)S(1)}, bf16[512,512]{1,0:T(8,128)(2,1)S(1)}, u32[]{:S(2)}, u32[]{:S(2)}) collective-permute-start(bf16[512,512]{1,0:T(8,128)(2,1)S(1)} %collective-permute-done.38.piece_ref), channel_id=1, source_target_pairs={{0,4},{8,0},{16,8},{24,16},{28,24},{20,28},{12,20},{4,12},{1,5},{9... | collective-permute-start | bytes 1572872 | tf_op jit(solution)/shard_map/ppermute | solution.py:211
  258.4 22.5 %collective-permute-start.49 = (bf16[512,512]{1,0:T(8,128)(2,1)S(1)}, bf16[512,512]{1,0:T(8,128)(2,1)S(1)}, u32[]{:S(2)}, u32[]{:S(2)}) collective-permute-start(bf16[512,512]{1,0:T(8,128)(2,1)S(1)} %collective-permute-done.45.piece_ref), channel_id=1, source_target_pairs={{0,8},{8,16},{16,24},{24,28},{28,20},{20,12},{12,4},{4,0},{1,9},{9... | collective-permute-start | bytes 1572872 | tf_op jit(solution)/shard_map/ppermute | solution.py:211
  264.6 22.5 %collective-permute-start.47 = (bf16[512,512]{1,0:T(8,128)(2,1)S(1)}, bf16[512,512]{1,0:T(8,128)(2,1)S(1)}, u32[]{:S(2)}, u32[]{:S(2)}) collective-permute-start(bf16[512,512]{1,0:T(8,128)(2,1)S(1)} %collective-permute-done.43.piece_ref), channel_id=1, source_target_pairs={{0,4},{8,0},{16,8},{24,16},{28,24},{20,28},{12,20},{4,12},{1,5},{9... | collective-permute-start | bytes 1572872 | tf_op jit(solution)/shard_map/ppermute | solution.py:211
  269.7 22.5 %collective-permute-start.48 = (bf16[512,512]{1,0:T(8,128)(2,1)S(1)}, bf16[512,512]{1,0:T(8,128)(2,1)S(1)}, u32[]{:S(2)}, u32[]{:S(2)}) collective-permute-start(bf16[512,512]{1,0:T(8,128)(2,1)S(1)} %collective-permute-done.44.piece_ref), channel_id=1, source_target_pairs={{0,8},{8,16},{16,24},{24,28},{28,20},{20,12},{12,4},{4,0},{1,9},{9... | collective-permute-start | bytes 1572872 | tf_op jit(solution)/shard_map/ppermute | solution.py:211
  275.8 22.5 %collective-permute-start.46 = (bf16[512,512]{1,0:T(8,128)(2,1)S(1)}, bf16[512,512]{1,0:T(8,128)(2,1)S(1)}, u32[]{:S(2)}, u32[]{:S(2)}) collective-permute-start(bf16[512,512]{1,0:T(8,128)(2,1)S(1)} %collective-permute-done.42.piece_ref), channel_id=1, source_target_pairs={{0,4},{8,0},{16,8},{24,16},{28,24},{20,28},{12,20},{4,12},{1,5},{9... | collective-permute-start | bytes 1572872 | tf_op jit(solution)/shard_map/ppermute | solution.py:211
  (40 other events, 747.7 us)
